TPU v7x, 32 devices: a whole 2x2x4 slice. The times are simulated.
32 devices in a mesh: wide: 8 (over y, x, core), narrow: 4 (over z).
Axes of the slice: x: 2, y: 2, z: 4, core: 2. Of those that a mesh axis runs over, the one named last changes fastest.
Arguments:
- heads_output: bfloat16 [512, 8192], P('narrow', 'wide'), may hold values from -6 to 6
- residual_in: bfloat16 [512, 16384], P('wide', 'narrow'), may hold values from -6 to 6
- out_weight: bfloat16 [8192, 16384], P('wide', 'narrow'), may hold values from -0.0625 to 0.0625
- norm_gain: float32 [16384], P('narrow'), may hold values from 0.1 to 1.9
- gate_weight: bfloat16 [16384, 26624], P('narrow', 'wide'), may hold values from -0.046875 to 0.046875
- up_weight: bfloat16 [16384, 26624], P('narrow', 'wide'), may hold values from -0.046875 to 0.046875
Outputs:
- residual: float32 [512, 16384], P('wide', 'narrow')
- hidden: float32 [512, 26624], P('narrow', 'wide')
All inputs are finite; a program needn't handle non-finite values.
Results may differ from a plain program's by a relative error of at most 0.0041.
Values may be sent and summed in bfloat16 or wider, within the bound.
No kernel may reach another device: no remote copies, remote signals or barrier semaphores. Data moves between devices by JAX's collectives and lax.ppermute only.
A program may use at most 128 MiB of HBM per device.

v0:
```python
import jax
import jax.numpy as jnp
from jax import lax
from jax.sharding import PartitionSpec as P

D = 16384


def norm_scale(squares):
    return 1.0 / jnp.sqrt(squares / D + 1e-05)


def on_device(heads_output, residual_in, out_weight, norm_gain, gate_weight, up_weight):
    gathered = lax.all_gather(heads_output, "narrow", axis=0, tiled=True)
    row_count = residual_in.shape[0]
    offset = lax.axis_index("wide") * row_count
    terms = jnp.dot(gathered, out_weight, preferred_element_type=jnp.float32)
    placed = lax.dynamic_update_slice_in_dim(
        jnp.zeros_like(terms), residual_in.astype(jnp.float32), offset, 0
    )
    total = lax.psum(terms + placed, "wide")
    squares = lax.psum(jnp.sum(total * total, axis=1), "narrow")
    normed = (total * norm_scale(squares)[:, None] * norm_gain).astype(jnp.bfloat16)
    residual = lax.dynamic_slice_in_dim(total, offset, row_count, 0)
    gate_part = jnp.dot(normed, gate_weight, preferred_element_type=jnp.float32)
    up_part = jnp.dot(normed, up_weight, preferred_element_type=jnp.float32)
    gate, up_sum = (
        lax.psum_scatter(gate_part, "narrow", scatter_dimension=0, tiled=True),
        lax.psum_scatter(up_part, "narrow", scatter_dimension=0, tiled=True),
    )
    hidden = jax.nn.silu(gate) * up_sum
    return (residual, hidden)


def solution(mesh):
    in_specs = (
        P("narrow", "wide"),
        P("wide", "narrow"),
        P("wide", "narrow"),
        P("narrow"),
        P("narrow", "wide"),
        P("narrow", "wide"),
    )
    out_specs = (P("wide", "narrow"), P("narrow", "wide"))
    return jax.shard_map(
        on_device, mesh=mesh, in_specs=in_specs, out_specs=out_specs, check_vma=False
    )
```

profile of v0, /device:TPU:0, one launch (start us, length us, event | category | flops | bytes accessed | tf_op | source)
XLA Modules:
  0.0 468.5 jit_solution(706944443829134367)
XLA Ops:
  7.2 0.0 all-gather.2.cloned.1.call-start
  7.2 0.7 all-gather.2.cloned.1.call-update
  7.9 0.0 all-reduce.2.cloned.1.call-start
  7.9 0.0 copy-start
  8.0 32.3 %all-gather.2.cloned.1.call-done = bf16[512,1024]{1,0:T(8,128)(2,1)} async-done(((bf16[128,1024]{1,0:T(8,128)(2,1)}), bf16[512,1024]{1,0:T(8,128)(2,1)}) %all-gather.2.cloned.1.call-update) | async-done | bytes 1048592 | tf_op jit(solution)/shard_map/all_gather | solution.py:14
  40.2 11.4 %fusion.2 = f32[512,4096]{1,0:T(8,128)} fusion(bf16[512,1024]{1,0:T(8,128)(2,1)} %all-gather.2.cloned.1.call-done, bf16[1024,4096]{1,0:T(8,128)(2,1)} %param.8), kind=kOutput, calls=%fused_computation.8 | convolution fusion | flops 4294967296 | bytes 17825792 | tf_op jit(solution)/shard_map/dot_general | solution.py:17
  51.7 0.0 copy-done
  51.7 2.4 add_dynamic-update-slice_fusion
  54.1 0.0 copy-start.1
  54.1 0.0 all-reduce.2.cloned.1.call-update
  54.1 0.0 reduce-scatter.5.cloned.1.call-start
  54.1 126.1 %all-reduce.2.cloned.1.call-done = f32[512,4096]{1,0:T(8,128)} async-done(((f32[512,4096]{1,0:T(8,128)}), f32[512,4096]{1,0:T(8,128)}) %all-reduce.2.cloned.1.call-update) | async-done | bytes 8388624 | tf_op jit(solution)/shard_map/psum | solution.py:21
  180.2 4.0 multiply_reduce_fusion
  184.2 11.7 %psum.15 = f32[512]{0:T(512)S(1)} all-reduce(f32[512]{0:T(512)S(1)} %multiply_reduce_fusion), channel_id=1, replica_groups=mesh['wide'=8,'narrow'=4] {'narrow'}, use_global_device_ids=true, to_apply=%region_2.0 | all-reduce | flops 512 | bytes 4096 | tf_op jit(solution)/shard_map/psum | solution.py:22
  195.9 0.0 copy-done.1
  195.9 23.6 %fusion = f32[512,3328]{1,0:T(8,128)} fusion(bf16[4096,3328]{1,0:T(8,128)(2,1)} %param.11, f32[512,4096]{1,0:T(8,128)} %all-reduce.2.cloned.1.call-done, f32[4096]{0:T(1024)S(1)} %copy-done.1, f32[512]{0:T(512)S(1)} %add_rsqrt_fusion), kind=kOutput, calls=%fused_computation.6 | convolution fusion | flops 13964935168 | bytes 42485760 | tf_op jit(solution)/shard_map/dot_general | solution.py:26
  219.5 0.0 reduce-scatter.5.cloned.1.call-update
  219.5 0.2 reduce-scatter.3.cloned.1.call-start
  219.7 24.8 %fusion.1 = f32[512,3328]{1,0:T(8,128)} fusion(bf16[4096,3328]{1,0:T(8,128)(2,1)} %param.10, f32[512,4096]{1,0:T(8,128)} %all-reduce.2.cloned.1.call-done, f32[4096]{0:T(1024)S(1)} %copy-done.1, f32[512]{0:T(512)S(1)} %add_rsqrt_fusion), kind=kOutput, calls=%fused_computation.7 | convolution fusion | flops 13964935168 | bytes 42485760 | tf_op jit(solution)/shard_map/dot_general | solution.py:25
  244.5 0.0 reduce-scatter.3.cloned.1.call-update
  244.5 2.3 constant_dynamic-slice_fusion
  246.9 89.5 %reduce-scatter.5.cloned.1.call-done = f32[128,3328]{1,0:T(8,128)} async-done(((f32[512,3328]{1,0:T(8,128)}), f32[128,3328]{1,0:T(8,128)}) %reduce-scatter.5.cloned.1.call-update) | async-done | bytes 1703952 | tf_op jit(solution)/shard_map/reduce_scatter | solution.py:29
  336.3 122.0 %reduce-scatter.3.cloned.1.call-done = f32[128,3328]{1,0:T(8,128)} async-done(((f32[512,3328]{1,0:T(8,128)}), f32[128,3328]{1,0:T(8,128)}) %reduce-scatter.3.cloned.1.call-update) | async-done | bytes 1703952 | tf_op jit(solution)/shard_map/reduce_scatter | solution.py:28
  458.4 3.6 multiply_multiply_fusion
  (1 shorter events, 0.0 us)
Async XLA Ops:
  7.2 33.1 %all-gather.2.cloned.1.call-start = ((), (), s32[]{:S(2)}) async-start(), calls=%async_computation.2 | async-start | bytes 1310720 | tf_op jit(solution)/shard_map/all_gather | solution.py:14
  7.9 172.3 %all-reduce.2.cloned.1.call-start = ((), (), s32[]{:S(2)}) async-start(), calls=%async_computation.3 | async-start | bytes 16777216 | tf_op jit(solution)/shard_map/psum | solution.py:21
  7.9 43.7 %copy-start = (bf16[64,4096]{1,0:T(8,128)(2,1)S(1)}, bf16[64,4096]{1,0:T(8,128)(2,1)}, u32[]{:S(2)}) copy-start(bf16[64,4096]{1,0:T(8,128)(2,1)} %param.7) | copy-start | bytes 1572868
  54.1 141.9 %copy-start.1 = (f32[4096]{0:T(1024)S(1)}, f32[4096]{0:T(1024)}, u32[]{:S(2)}) copy-start(f32[4096]{0:T(1024)} %param.9) | copy-start | bytes 49156
  54.1 282.2 %reduce-scatter.5.cloned.1.call-start = ((), (), s32[]{:S(2)}) async-start(), calls=%async_computation.5 | async-start | bytes 8519680 | tf_op jit(solution)/shard_map/reduce_scatter | solution.py:29
  219.5 238.9 %reduce-scatter.3.cloned.1.call-start = ((), (), s32[]{:S(2)}) async-start(), calls=%async_computation.4 | async-start | bytes 8519680 | tf_op jit(solution)/shard_map/reduce_scatter | solution.py:28
Sparse Core Ops, SparseCore 0:
  9.6 30.6 all-gather.1
  54.2 125.9 all-reduce.1
  219.6 116.6 reduce-scatter.4
  338.6 119.7 reduce-scatter.2
where the time goes:
time: 469 us
  waiting for transfers between devices  371 us (79%)
  matrix products  59.8 us (13%)
  between operations  13.8 us (3%)
  blocking collectives  11.7 us (2%)
  other arithmetic  10 us (2%)
    psum x1, waiting for transfers between devices, on_device(): total = lax.psum(terms + placed, 'wide')  126 us
    reduce_scatter x1, waiting for transfers between devices, on_device(): lax.psum_scatter(gate_part, 'narrow', scatter_dimension=0, tiled=True)  122 us
    reduce_scatter x1, waiting for transfers between devices, on_device(): lax.psum_scatter(up_part, 'narrow', scatter_dimension=0, tiled=True)  89.5 us
    all_gather x1, waiting for transfers between devices, on_device(): gathered = lax.all_gather(heads_output, 'narrow', axis=0, tiled=True)  32.3 us
    dot_general x1, matrix products, on_device(): gate_part = jnp.dot(normed, gate_weight, preferred_element_type=jnp.float32)  24.8 us
    dot_general x1, matrix products, on_device(): up_part = jnp.dot(normed, up_weight, preferred_element_type=jnp.float32)  23.6 us
    psum x1, blocking collectives, on_device(): squares = lax.psum(jnp.sum(total * total, axis=1), 'narrow')  11.7 us
    dot_general x1, matrix products, on_device(): terms = jnp.dot(gathered, out_weight, preferred_element_type=jnp.float32)  11.4 us
  transfers between devices with their start and end apart: 4, of which 4 were waited for; matrix products, arithmetic and copies ran while one was open for 6% of the time, Pallas kernels for 0%

commit v1 on v0

v1 whole, which is shorter than its diff:
```python
import jax
import jax.numpy as jnp
from jax import lax
from jax.sharding import PartitionSpec as P

F32, BF16 = jnp.float32, jnp.bfloat16
SHARES = (32, 32)


def pick(value, index, axis=0):
    return lax.dynamic_index_in_dim(value, index, axis, keepdims=False)


def tie(value, after):
    return lax.optimization_barrier((value, after))[0] if after else value


def solution(mesh):
    wide, narrow = mesh.shape["wide"], mesh.shape["narrow"]
    chips = wide // 2
    assert chips == narrow

    def swap(value, bits):
        return lax.ppermute(value, "wide", [(i, i ^ bits) for i in range(wide)])

    def shift(value, by):
        return lax.ppermute(value, "narrow", [(i, (i + by) % narrow) for i in range(narrow)])

    def hop(value, step):
        pairs = [(step - 1, step), (narrow - step, narrow - 1 - step)]
        return lax.ppermute(value, "narrow", pairs)

    def on_device(heads_output, residual_in, out_weight, norm_gain, gate_weight, up_weight):
        me, place = lax.axis_index("wide"), lax.axis_index("narrow")
        chip, core = me // 2, me % 2
        rows, width = residual_in.shape
        features = width * narrow
        depth = heads_output.shape[1]
        heads = heads_output.reshape(2, rows, depth)

        def fetch(at, share, after):
            own = tie(heads[:, at : at + share], after)
            return jnp.stack([own] + [shift(own, s) for s in range(1, narrow)])

        def project(stacked):
            share = stacked.shape[2]

            def terms(which):
                left = pick(stacked, which, 1).reshape(narrow * share, depth)
                return jnp.dot(left, out_weight, preferred_element_type=F32)

            sent = terms(1 - core)
            got = swap(sent, 1)
            kept, _ = lax.optimization_barrier((terms(core), sent))
            return kept, got

        def spread(kept, got):
            total = (kept + got).reshape(narrow, -1, width)

            def for_chip(d):
                return pick(total, (place - (chip ^ d)) % narrow)

            return for_chip(0), [swap(for_chip(d), 2 * d) for d in range(1, chips)]

        def scale_of(residual, after):
            own = jnp.sum(residual * residual, axis=1)
            others = tie([shift(own, s) for s in range(1, narrow)], after)
            return 1.0 / jnp.sqrt(sum(others, own) / features + 1e-05)

        def gather(normed, after):
            return jnp.stack([normed] + tie([swap(normed, 2 * d) for d in range(1, chips)], after))

        def both(near):
            near = jnp.stack([pick(near, j ^ chip) for j in range(chips)])
            return jnp.stack([near, swap(near, 1)], 1)

        def multiply(all_rows, weight, after):
            left = tie(all_rows.reshape(-1, width), after)
            terms = jnp.dot(left, weight, preferred_element_type=F32)
            return terms.reshape(*all_rows.shape[:-1], -1)

        def reduce_call(terms):
            return lax.psum_scatter(terms.astype(BF16), "narrow", scatter_dimension=0, tiled=True)

        def staged_sums(gate, up, beside):
            terms = (gate, up)
            far = narrow - 1
            items = [(0, far)]
            for b in range(far - 1, -1, -1):
                items += ([(0, b)] if b else []) + [(1, b + 1)]
            waiting = [items[:1]] + [items[i : i + 2] for i in range(1, len(items), 2)]
            totals = [pick(t, place) for t in terms]
            flying, stage = [], 0
            while waiting or flying:
                entering = waiting.pop(0) if waiting else []
                lanes = {}
                for which, b, step, carried in flying + [(which, b, 0, 0.0) for which, b in entering]:
                    index = jnp.where(place == step, b, narrow - 1 - b)
                    part = (pick(terms[which], index) + carried).astype(BF16)
                    lanes.setdefault(step + 1, []).append((which, b, part))
                moved = {step: hop(jnp.stack([part for _, _, part in lane]), step) for step, lane in lanes.items()}
                moved, _ = lax.optimization_barrier((moved, beside[stage] if stage < len(beside) else ()))
                stage += 1
                flying = []
                for step, lane in lanes.items():
                    for (which, b, _), value in zip(lane, moved[step]):
                        if step == b:
                            totals[which] = totals[which] + value
                        else:
                            flying.append((which, b, step, value))
            return totals

        first, second = SHARES
        stacked_a = fetch(0, first, ())
        kept_a, got_a = project(stacked_a)
        whole = lax.all_gather(tie(heads, (stacked_a,)), "narrow", axis=0)
        own_a, parts_a = spread(kept_a, got_a)
        stacked_b = jnp.stack([pick(whole, (place - s) % narrow) for s in range(narrow)])[:, :, first:]
        residual_a = residual_in[:first].astype(F32) + sum(parts_a, own_a)
        scale_a = scale_of(residual_a, ())
        normed_a = (residual_a * scale_a[:, None] * norm_gain).astype(BF16)
        kept_b, got_b = project(tie(stacked_b, (normed_a,)))
        near_a = gather(normed_a, (kept_b,))
        rows_a = both(near_a)

        own_b, parts_b = spread(tie(kept_b, (near_a,)), got_b)
        gate_a = multiply(rows_a, gate_weight, ())
        gate_sum_a = reduce_call(gate_a)
        parts_b = tie(parts_b, (gate_a,))
        residual_b = residual_in[first:].astype(F32) + sum(parts_b, own_b)
        scale_b = scale_of(residual_b, ())
        normed_b = (residual_b * scale_b[:, None] * norm_gain).astype(BF16)
        up_a = multiply(rows_a, up_weight, (gate_a, normed_b))
        up_sum_a = reduce_call(up_a)
        rows_b = both(gather(normed_b, (up_a,)))
        gate_b = multiply(rows_b, gate_weight, (gate_sum_a,))
        up_b = multiply(rows_b, up_weight, (gate_b,))
        gate_sum_b, up_sum_b = staged_sums(gate_b, up_b, ((up_b,), (up_sum_a,)))

        residuals = [residual_a, residual_b]
        outs = []
        for gate, up in ((gate_sum_a[0], up_sum_a[0]), (gate_sum_b, up_sum_b)):
            hidden = jax.nn.silu(gate.astype(F32)) * up.astype(F32)
            outs.append(jnp.where(core == 0, hidden, hidden[::-1]))
        hidden = jnp.concatenate(outs, axis=1)
        return jnp.concatenate(residuals, axis=0), hidden.reshape(2 * rows, -1)

    in_specs = (
        P("narrow", "wide"),
        P("wide", "narrow"),
        P("wide", "narrow"),
        P("narrow"),
        P("narrow", "wide"),
        P("narrow", "wide"),
    )
    out_specs = (P("wide", "narrow"), P("narrow", "wide"))
    return jax.shard_map(on_device, mesh=mesh, in_specs=in_specs, out_specs=out_specs, check_vma=False)
```

time: 469 us -> 266 us (0.57)
  waiting for transfers between devices: 371 us -> 102 us
  starting transfers between devices: 0.34 us -> 50.4 us
  blocking collectives: 11.7 us -> 0 us
  matrix products: 59.8 us -> 70 us
  other arithmetic: 10 us -> 18.4 us
  local copies, waits for them, and re-layouts: 2.34 us -> 9.24 us
    reduce_scatter x2, waiting for transfers between devices: 212 us -> 0.01 us  [reduce_call(): lax.psum_scatter(terms.astype(BF16), 'narrow', scatter_dimension=0, tiled...]
    psum x1 -> x0, waiting for transfers between devices: 126 us -> none  [on_device(): total = lax.psum(terms + placed, 'wide')]
    ppermute x0 -> x34, waiting for transfers between devices: none -> 83.7 us  [the longest x9 53.7 us: hop(): return lax.ppermute(value, 'narrow', pairs)]
    ppermute x0 -> x34, starting transfers between devices: none -> 50.1 us  [the longest x9 19.8 us: hop(): return lax.ppermute(value, 'narrow', pairs)]
    all_gather x1, waiting for transfers between devices: 32.3 us -> 18.6 us  [on_device(): whole = lax.all_gather(tie(heads, (stacked_a,)), 'narrow', axis=0)]
    psum x1 -> x0, blocking collectives: 11.7 us -> none  [on_device(): squares = lax.psum(jnp.sum(total * total, axis=1), 'narrow')]
    dot_general x3 -> x8, matrix products: 59.8 us -> 70 us  [the longest x4 54.5 us: multiply(): terms = jnp.dot(left, weight, preferred_element_type=F32)]
    another operation x0 -> x13, other arithmetic: none -> 5.35 us  [the longest x4 3.56 us: both(): return jnp.stack([near, swap(near, 1)], 1)]
  transfers between devices with their start and end apart: 4 -> 37, of which waited for: 4 -> 17; matrix products, arithmetic and copies ran while one was open for 6% -> 32% of each run, Pallas kernels for 0% -> 0%
where the time goes in v1:
time: 266 us; the launch traced here: 265 us
  waiting for transfers between devices  102 us (38%)
  matrix products  70 us (26%)
  starting transfers between devices  50.4 us (19%)
  other arithmetic  18.4 us (7%)
  between operations  14.4 us (5%)
  local copies, waits for them, and re-layouts  9.24 us (3%)
    dot_general x4, matrix products, multiply(): terms = jnp.dot(left, weight, preferred_element_type=F32)  54.5 us
    ppermute x9, waiting for transfers between devices, hop(): return lax.ppermute(value, 'narrow', pairs)  53.7 us
    ppermute x9, starting transfers between devices, hop(): return lax.ppermute(value, 'narrow', pairs)  19.8 us
    all_gather x1, waiting for transfers between devices, on_device(): whole = lax.all_gather(tie(heads, (stacked_a,)), 'narrow', axis=0)  18.6 us
    ppermute x9, starting transfers between devices, shift(): lax.ppermute(value, 'narrow', [(i, (i + by) % narrow) for i in range(narr...  15.9 us
    dot_general x4, matrix products, terms(): return jnp.dot(left, out_weight, preferred_element_type=F32)  15.4 us
    ppermute x9, waiting for transfers between devices, shift(): lax.ppermute(value, 'narrow', [(i, (i + by) % narrow) for i in range(narr...  15.3 us
    ppermute x16, waiting for transfers between devices, swap(): return lax.ppermute(value, 'wide', [(i, i ^ bits) for i in range(wide)])  14.7 us
  transfers between devices with their start and end apart: 37, of which 17 were waited for; matrix products, arithmetic and copies ran while one was open for 32% of the time, Pallas kernels for 0%

profile of v1, /device:TPU:0, one launch (start us, length us, event | category | flops | bytes accessed | tf_op | source)
XLA Modules:
  0.0 264.7 jit_solution(7666460678538637240)
XLA Ops:
  7.2 0.9 slice_bitcast_fusion
  8.1 4.1 %collective-permute-start.1 = (bf16[2,32,1024]{2,1,0:T(8,128)(2,1)S(1)}, bf16[2,32,1024]{2,1,0:T(8,128)(2,1)S(1)}, u32[]{:S(2)}, u32[]{:S(2)}) collective-permute-start(bf16[2,32,1024]{2,1,0:T(8,128)(2,1)S(1)} %get-tuple-element.96), channel_id=1, source_target_pairs={{0,2},{1,3},{2,0},{3,1},{4,6},{5,7},{6,4},{7,5},{8,10},{9,11},{10,... | collective-permute-start | bytes 393224 | tf_op jit(solution)/shard_map/ppermute | solution.py:27
  12.2 1.6 collective-permute-start
  13.8 2.2 collective-permute-start.2
  16.1 6.2 %collective-permute-done.1 = bf16[2,32,1024]{2,1,0:T(8,128)(2,1)S(1)} collective-permute-done((bf16[2,32,1024]{2,1,0:T(8,128)(2,1)S(1)}, bf16[2,32,1024]{2,1,0:T(8,128)(2,1)S(1)}, u32[]{:S(2)}, u32[]{:S(2)}) %collective-permute-start.1) | collective-permute-done | bytes 131104 | tf_op jit(solution)/shard_map/ppermute | solution.py:27
  23.1 4.7 %fusion.20 = f32[128,4096]{1,0:T(8,128)S(1)} fusion(bf16[128,1024]{1,0:T(8,128)(2,1)S(1)} %bitcast.129, bf16[1024,4096]{1,0:T(8,128)(2,1)} %param.8), kind=kOutput, calls=%fused_computation.83 | convolution fusion | flops 1073741824 | bytes 10747904 | tf_op jit(solution)/shard_map/dot_general | solution.py:50
  28.0 4.7 %fusion.19 = f32[128,4096]{1,0:T(8,128)S(1)} fusion(bf16[128,1024]{1,0:T(8,128)(2,1)S(1)} %bitcast.126, bf16[1024,4096]{1,0:T(8,128)(2,1)} %param.8), kind=kOutput, calls=%fused_computation.82 | convolution fusion | flops 1073741824 | bytes 10747904 | tf_op jit(solution)/shard_map/dot_general | solution.py:50
  32.7 1.9 add.231
  34.6 0.9 dynamic-slice_bitcast_fusion.5
  35.5 1.5 collective-permute-start.4
  37.1 1.5 collective-permute-start.6
  39.0 18.6 %all-gather.3.cloned.1.call-done = bf16[8,64,1024]{2,1,0:T(8,128)(2,1)} async-done(((bf16[2,64,1024]{2,1,0:T(8,128)(2,1)}), bf16[8,64,1024]{2,1,0:T(8,128)(2,1)}) %all-gather.3.cloned.1.call-update) | async-done | bytes 1048592 | tf_op jit(solution)/shard_map/all_gather | solution.py:116
  57.6 1.3 constant_dynamic-slice_fusion.13
  59.0 3.5 %collective-permute-done.6 = f32[32,4096]{1,0:T(8,128)} collective-permute-done((f32[32,4096]{1,0:T(8,128)S(1)}, f32[32,4096]{1,0:T(8,128)}, u32[]{:S(2)}, u32[]{:S(2)}) %collective-permute-start.6) | collective-permute-done | bytes 524320 | tf_op jit(solution)/shard_map/ppermute | solution.py:24
  62.5 1.2 collective-permute-done.5
  63.6 1.6 multiply_reduce_fusion.1
  65.2 2.1 collective-permute-start.9
  67.3 1.9 collective-permute-start.8
  69.2 1.9 collective-permute-start.7
  71.7 2.8 %collective-permute-done.7 = f32[32]{0:T(128)S(1)} collective-permute-done((f32[32]{0:T(128)S(1)}, f32[32]{0:T(128)S(1)}, u32[]{:S(2)}, u32[]{:S(2)}) %collective-permute-start.7) | collective-permute-done | bytes 160 | tf_op jit(solution)/shard_map/ppermute | solution.py:27
  75.3 1.5 collective-permute-start.10
  76.8 1.5 collective-permute-start.12
  78.4 4.8 %fusion.22 = f32[128,4096]{1,0:T(8,128)S(1)} fusion(bf16[128,1024]{1,0:T(8,128)(2,1)S(1)} %bitcast.128, bf16[1024,4096]{1,0:T(8,128)(2,1)} %param.8), kind=kOutput, calls=%fused_computation.85 | convolution fusion | flops 1073741824 | bytes 10747904 | tf_op jit(solution)/shard_map/dot_general | solution.py:50
  83.3 0.9 slice-done.1
  84.2 1.3 fusion.21
  85.5 2.0 collective-permute-done.12
  88.2 1.2 dynamic-slice_bitcast_fusion
  89.4 1.4 collective-permute-start.16
  90.8 1.5 collective-permute-start.15
  92.9 1.0 copy-done.4
  93.9 13.8 %fusion = bf16[4,2,32,3328]{3,2,1,0:T(8,128)(2,1)} fusion(bf16[4096,3328]{1,0:T(8,128)(2,1)} %param.10, bf16[4,1,32,4096]{3,2,1,0:T(8,128)(2,1)S(1)} %bitcast.131, bf16[4,1,32,4096]{3,2,1,0:T(8,128)(2,1)S(1)} %get-tuple-element.80), kind=kOutput, calls=%fused_computation | convolution fusion | flops 6980370432 | bytes 31064064 | tf_op jit(solution)/shard_map/dot_general | solution.py:79
  107.9 1.8 pad_maximum_fusion
  109.8 6.4 %collective-permute-done.15 = f32[32,4096]{1,0:T(8,128)} collective-permute-done((f32[32,4096]{1,0:T(8,128)}, f32[32,4096]{1,0:T(8,128)}, u32[]{:S(2)}, u32[]{:S(2)}) %collective-permute-start.15) | collective-permute-done | bytes 524320 | tf_op jit(solution)/shard_map/ppermute | solution.py:24
  116.2 1.6 multiply_reduce_fusion
  118.3 0.9 collective-permute-start.19
  119.9 1.7 collective-permute-done.20
  121.5 1.4 collective-permute-done.19
  123.0 1.9 collective-permute-done.18
  125.4 1.5 collective-permute-start.21
  126.9 1.7 collective-permute-start.23
  128.6 13.9 %fusion.23 = bf16[256,3328]{1,0:T(8,128)(2,1)} fusion(bf16[256,4096]{1,0:T(8,128)(2,1)S(1)} %bitcast.121, bf16[4096,3328]{1,0:T(8,128)(2,1)} %param.11), kind=kOutput, calls=%fused_computation.86 | convolution fusion | flops 6979321856 | bytes 31064064 | tf_op jit(solution)/shard_map/dot_general | solution.py:79
  143.1 1.0 pad_maximum_fusion.5
  144.2 1.7 collective-permute-done.24
  145.9 1.4 pad_maximum_fusion.1
  147.3 1.5 copy.12
  148.8 13.8 %fusion.24 = f32[256,3328]{1,0:T(8,128)S(1)} fusion(bf16[256,4096]{1,0:T(8,128)(2,1)} %bitcast.122, bf16[4096,3328]{1,0:T(8,128)(2,1)} %param.10), kind=kOutput, calls=%fused_computation.87 | convolution fusion | flops 6979321856 | bytes 32768000 | tf_op jit(solution)/shard_map/dot_general | solution.py:79
  162.7 1.7 collective-permute-start.27
  164.5 13.1 %fusion.25 = f32[256,3328]{1,0:T(8,128)S(1)} fusion(bf16[256,4096]{1,0:T(8,128)(2,1)S(1)} %bitcast.123, bf16[4096,3328]{1,0:T(8,128)(2,1)} %param.11), kind=kOutput, calls=%fused_computation.88 | convolution fusion | flops 6979321856 | bytes 32768000 | tf_op jit(solution)/shard_map/dot_general | solution.py:79
  177.6 1.1 dynamic-slice_convert_fusion.2
  178.7 2.1 collective-permute-start.31
  180.9 2.2 collective-permute-start.26
  183.6 1.5 collective-permute-start.28
  185.1 1.0 pad_maximum_fusion.8
  186.1 8.1 %collective-permute-start.25 = (bf16[2,2,32,3328]{3,2,1,0:T(8,128)(2,1)}, bf16[2,2,32,3328]{3,2,1,0:T(8,128)(2,1)}, u32[]{:S(2)}, u32[]{:S(2)}) collective-permute-start(bf16[2,2,32,3328]{3,2,1,0:T(8,128)(2,1)} %pad_maximum_fusion.8), channel_id=1, source_target_pairs={{0,1},{3,2},{4,5},{7,6},{8,9},{11,10},{12,13},{15,14},{16,17},{19,... | collective-permute-start | bytes 2555912 | tf_op jit(solution)/shard_map/ppermute | solution.py:31
  194.2 20.4 %collective-permute-done.26 = bf16[2,2,32,3328]{3,2,1,0:T(8,128)(2,1)} collective-permute-done((bf16[2,2,32,3328]{3,2,1,0:T(8,128)(2,1)S(1)}, bf16[2,2,32,3328]{3,2,1,0:T(8,128)(2,1)}, u32[]{:S(2)}, u32[]{:S(2)}) %collective-permute-start.26) | collective-permute-done | bytes 852000 | tf_op jit(solution)/shard_map/ppermute | solution.py:31
  214.6 1.8 add_convert_fusion.2
  216.4 1.6 collective-permute-start.30
  218.1 0.7 collective-permute-start.29
  219.1 13.7 %collective-permute-done.25 = bf16[2,2,32,3328]{3,2,1,0:T(8,128)(2,1)} collective-permute-done((bf16[2,2,32,3328]{3,2,1,0:T(8,128)(2,1)}, bf16[2,2,32,3328]{3,2,1,0:T(8,128)(2,1)}, u32[]{:S(2)}, u32[]{:S(2)}) %collective-permute-start.25) | collective-permute-done | bytes 852000 | tf_op jit(solution)/shard_map/ppermute | solution.py:31
  232.8 1.2 add_convert_fusion
  234.0 1.3 collective-permute-start.33
  236.0 19.1 %collective-permute-done.33 = bf16[1,2,32,3328]{3,2,1,0:T(8,128)(2,1)S(1)} collective-permute-done((bf16[1,2,32,3328]{3,2,1,0:T(8,128)(2,1)S(1)}, bf16[1,2,32,3328]{3,2,1,0:T(8,128)(2,1)S(1)}, u32[]{:S(2)}, u32[]{:S(2)}) %collective-permute-start.33) | collective-permute-done | bytes 426016 | tf_op jit(solution)/shard_map/ppermute | solution.py:31
  255.1 1.7 bitcast_multiply_fusion
  256.9 1.3 pad_maximum_fusion.2
  (87 shorter events, 8.7 us)
Async XLA Ops:
  7.2 50.5 %all-gather.3.cloned.1.call-start = ((), (), s32[]{:S(2)}) async-start(), calls=%async_computation.4 | async-start | bytes 1310720 | tf_op jit(solution)/shard_map/all_gather | solution.py:116
  8.1 14.1 %collective-permute-start.1 = (bf16[2,32,1024]{2,1,0:T(8,128)(2,1)S(1)}, bf16[2,32,1024]{2,1,0:T(8,128)(2,1)S(1)}, u32[]{:S(2)}, u32[]{:S(2)}) collective-permute-start(bf16[2,32,1024]{2,1,0:T(8,128)(2,1)S(1)} %get-tuple-element.96), channel_id=1, source_target_pairs={{0,2},{1,3},{2,0},{3,1},{4,6},{5,7},{6,4},{7,5},{8,10},{9,11},{10,... | collective-permute-start | bytes 393224 | tf_op jit(solution)/shard_map/ppermute | solution.py:27
  12.2 10.0 %collective-permute-start = (bf16[2,32,1024]{2,1,0:T(8,128)(2,1)S(1)}, bf16[2,32,1024]{2,1,0:T(8,128)(2,1)S(1)}, u32[]{:S(2)}, u32[]{:S(2)}) collective-permute-start(bf16[2,32,1024]{2,1,0:T(8,128)(2,1)S(1)} %get-tuple-element.96), channel_id=1, source_target_pairs={{0,1},{1,2},{2,3},{3,0},{4,5},{5,6},{6,7},{7,4},{8,9},{9,10},{10,1... | collective-permute-start | bytes 393224 | tf_op jit(solution)/shard_map/ppermute | solution.py:27
  13.8 9.1 %collective-permute-start.2 = (bf16[2,32,1024]{2,1,0:T(8,128)(2,1)S(1)}, bf16[2,32,1024]{2,1,0:T(8,128)(2,1)S(1)}, u32[]{:S(2)}, u32[]{:S(2)}) collective-permute-start(bf16[2,32,1024]{2,1,0:T(8,128)(2,1)S(1)} %get-tuple-element.96), channel_id=1, source_target_pairs={{0,3},{1,0},{2,1},{3,2},{4,7},{5,4},{6,5},{7,6},{8,11},{9,8},{10,9... | collective-permute-start | bytes 393224 | tf_op jit(solution)/shard_map/ppermute | solution.py:27
  27.8 4.9 %collective-permute-start.3 = (f32[128,4096]{1,0:T(8,128)S(1)}, f32[128,4096]{1,0:T(8,128)}, u32[]{:S(2)}, u32[]{:S(2)}) collective-permute-start(f32[128,4096]{1,0:T(8,128)S(1)} %fusion.20), channel_id=1, source_target_pairs={{0,4},{4,0},{8,12},{12,8},{16,20},{20,16},{24,28},{28,24},{1,5},{5... | collective-permute-start | bytes 6291464 | tf_op jit(solution)/shard_map/ppermute | solution.py:24
  27.9 120.9 %reduce-scatter.3.cloned.1.call-start = ((), (), s32[]{:S(2)}) async-start(), calls=%async_computation.2 | async-start | bytes 2129920 | tf_op jit(solution)/shard_map/reduce_scatter | solution.py:83
  35.5 23.5 %collective-permute-start.4 = (f32[32,4096]{1,0:T(8,128)}, f32[32,4096]{1,0:T(8,128)}, u32[]{:S(2)}, u32[]{:S(2)}) collective-permute-start(f32[32,4096]{1,0:T(8,128)} %get-tuple-element.71), channel_id=1, source_target_pairs={{0,8},{4,12},{8,0},{12,4},{16,24},{20,28},{24,16},{28,20},{1,9},{5... | collective-permute-start | bytes 1572872 | tf_op jit(solution)/shard_map/ppermute | solution.py:24
  37.1 25.4 %collective-permute-start.6 = (f32[32,4096]{1,0:T(8,128)S(1)}, f32[32,4096]{1,0:T(8,128)}, u32[]{:S(2)}, u32[]{:S(2)}) collective-permute-start(f32[32,4096]{1,0:T(8,128)S(1)} %get-tuple-element.72), channel_id=1, source_target_pairs={{0,24},{4,28},{8,16},{12,20},{16,8},{20,12},{24,0},{28,4},{1,25},{... | collective-permute-start | bytes 1572872 | tf_op jit(solution)/shard_map/ppermute | solution.py:24
  38.5 25.1 %collective-permute-start.5 = (f32[32,4096]{1,0:T(8,128)S(1)}, f32[32,4096]{1,0:T(8,128)}, u32[]{:S(2)}, u32[]{:S(2)}) collective-permute-start(f32[32,4096]{1,0:T(8,128)S(1)} %get-tuple-element.73), channel_id=1, source_target_pairs={{0,16},{4,20},{8,24},{12,28},{16,0},{20,4},{24,8},{28,12},{1,17},{... | collective-permute-start | bytes 1572872 | tf_op jit(solution)/shard_map/ppermute | solution.py:24
  57.6 6.0 %copy-start.5 = (bf16[64,4096]{1,0:T(8,128)(2,1)S(1)}, bf16[64,4096]{1,0:T(8,128)(2,1)}, u32[]{:S(2)}) copy-start(bf16[64,4096]{1,0:T(8,128)(2,1)} %param.7) | copy-start | bytes 1572868
  58.9 15.6 %copy-start.9 = (f32[4096]{0:T(1024)S(1)}, f32[4096]{0:T(1024)}, u32[]{:S(2)}) copy-start(f32[4096]{0:T(1024)} %param.9) | copy-start | bytes 49156
  65.2 5.9 %collective-permute-start.9 = (f32[32]{0:T(128)S(1)}, f32[32]{0:T(128)S(1)}, u32[]{:S(2)}, u32[]{:S(2)}) collective-permute-start(f32[32]{0:T(128)S(1)} %get-tuple-element.56), channel_id=1, source_target_pairs={{0,3},{1,0},{2,1},{3,2},{4,7},{5,4},{6,5},{7,6},{8,11},{9,8},{10,9... | collective-permute-start | bytes 392 | tf_op jit(solution)/shard_map/ppermute | solution.py:27
  67.3 4.4 %collective-permute-start.8 = (f32[32]{0:T(128)S(1)}, f32[32]{0:T(128)S(1)}, u32[]{:S(2)}, u32[]{:S(2)}) collective-permute-start(f32[32]{0:T(128)S(1)} %get-tuple-element.56), channel_id=1, source_target_pairs={{0,2},{1,3},{2,0},{3,1},{4,6},{5,7},{6,4},{7,5},{8,10},{9,11},{10,... | collective-permute-start | bytes 392 | tf_op jit(solution)/shard_map/ppermute | solution.py:27
  69.2 5.3 %collective-permute-start.7 = (f32[32]{0:T(128)S(1)}, f32[32]{0:T(128)S(1)}, u32[]{:S(2)}, u32[]{:S(2)}) collective-permute-start(f32[32]{0:T(128)S(1)} %get-tuple-element.56), channel_id=1, source_target_pairs={{0,1},{1,2},{2,3},{3,0},{4,5},{5,6},{6,7},{7,4},{8,9},{9,10},{10,1... | collective-permute-start | bytes 392 | tf_op jit(solution)/shard_map/ppermute | solution.py:27
  74.8 10.7 %collective-permute-start.11 = (bf16[32,4096]{1,0:T(8,128)(2,1)S(1)}, bf16[32,4096]{1,0:T(8,128)(2,1)S(1)}, u32[]{:S(2)}, u32[]{:S(2)}) collective-permute-start(bf16[32,4096]{1,0:T(8,128)(2,1)S(1)} %multiply_convert_fusion.1), channel_id=1, source_target_pairs={{0,16},{4,20},{8,24},{12,28},{16,0},{20,4},{24,8},{28,12},{1,17},{... | collective-permute-start | bytes 786440 | tf_op jit(solution)/shard_map/ppermute | solution.py:24
  75.3 10.1 %collective-permute-start.10 = (bf16[32,4096]{1,0:T(8,128)(2,1)S(1)}, bf16[32,4096]{1,0:T(8,128)(2,1)S(1)}, u32[]{:S(2)}, u32[]{:S(2)}) collective-permute-start(bf16[32,4096]{1,0:T(8,128)(2,1)S(1)} %multiply_convert_fusion.1), channel_id=1, source_target_pairs={{0,8},{4,12},{8,0},{12,4},{16,24},{20,28},{24,16},{28,20},{1,9},{5... | collective-permute-start | bytes 786440 | tf_op jit(solution)/shard_map/ppermute | solution.py:24
  76.8 10.7 %collective-permute-start.12 = (bf16[32,4096]{1,0:T(8,128)(2,1)S(1)}, bf16[32,4096]{1,0:T(8,128)(2,1)S(1)}, u32[]{:S(2)}, u32[]{:S(2)}) collective-permute-start(bf16[32,4096]{1,0:T(8,128)(2,1)S(1)} %multiply_convert_fusion.1), channel_id=1, source_target_pairs={{0,24},{4,28},{8,16},{12,20},{16,8},{20,12},{24,0},{28,4},{1,25},{... | collective-permute-start | bytes 786440 | tf_op jit(solution)/shard_map/ppermute | solution.py:24
  78.3 4.9 %slice-start = ((s8[8388608]{0:T(1024)(128)(4,1)}), s8[4194304]{0:T(1024)(128)(4,1)S(1)}, s32[]{:S(2)}) async-start(s8[8388608]{0:T(1024)(128)(4,1)} %bitcast.107), calls=%async_computation.5 | async-start | bytes 8388608
  78.4 5.8 %slice-start.1 = ((s8[8388608]{0:T(1024)(128)(4,1)}), s8[4194304]{0:T(1024)(128)(4,1)S(1)}, s32[]{:S(2)}) async-start(s8[8388608]{0:T(1024)(128)(4,1)} %bitcast.107), calls=%async_computation.6 | async-start | bytes 8388608
  83.2 4.8 %collective-permute-start.13 = (f32[128,4096]{1,0:T(8,128)S(1)}, f32[128,4096]{1,0:T(8,128)S(1)}, u32[]{:S(2)}, u32[]{:S(2)}) collective-permute-start(f32[128,4096]{1,0:T(8,128)S(1)} %fusion.22), channel_id=1, source_target_pairs={{0,4},{4,0},{8,12},{12,8},{16,20},{20,16},{24,28},{28,24},{1,5},{5... | collective-permute-start | bytes 6291464 | tf_op jit(solution)/shard_map/ppermute | solution.py:24
  87.9 5.0 %copy-start.2 = (bf16[4,1,32,4096]{3,2,1,0:T(8,128)(2,1)}, bf16[4,1,32,4096]{3,2,1,0:T(8,128)(2,1)S(1)}, u32[]{:S(2)}) copy-start(bf16[4,1,32,4096]{3,2,1,0:T(8,128)(2,1)S(1)} %get-tuple-element.80) | copy-start | bytes 3145732
  87.9 5.0 %collective-permute-start.17 = (bf16[4,32,4096]{2,1,0:T(8,128)(2,1)S(1)}, bf16[4,32,4096]{2,1,0:T(8,128)(2,1)S(1)}, u32[]{:S(2)}, u32[]{:S(2)}) collective-permute-start(bf16[4,32,4096]{2,1,0:T(8,128)(2,1)S(1)} %get-tuple-element.81), channel_id=1, source_target_pairs={{0,4},{4,0},{8,12},{12,8},{16,20},{20,16},{24,28},{28,24},{1,5},{5... | collective-permute-start | bytes 3145736 | tf_op jit(solution)/shard_map/ppermute | solution.py:24
  89.4 20.3 %collective-permute-start.16 = (f32[32,4096]{1,0:T(8,128)}, f32[32,4096]{1,0:T(8,128)}, u32[]{:S(2)}, u32[]{:S(2)}) collective-permute-start(f32[32,4096]{1,0:T(8,128)} %get-tuple-element.68), channel_id=1, source_target_pairs={{0,24},{4,28},{8,16},{12,20},{16,8},{20,12},{24,0},{28,4},{1,25},{... | collective-permute-start | bytes 1572872 | tf_op jit(solution)/shard_map/ppermute | solution.py:24
  90.8 25.3 %collective-permute-start.15 = (f32[32,4096]{1,0:T(8,128)}, f32[32,4096]{1,0:T(8,128)}, u32[]{:S(2)}, u32[]{:S(2)}) collective-permute-start(f32[32,4096]{1,0:T(8,128)} %get-tuple-element.69), channel_id=1, source_target_pairs={{0,16},{4,20},{8,24},{12,28},{16,0},{20,4},{24,8},{28,12},{1,17},{... | collective-permute-start | bytes 1572872 | tf_op jit(solution)/shard_map/ppermute | solution.py:24
  92.4 23.8 %collective-permute-start.14 = (f32[32,4096]{1,0:T(8,128)S(1)}, f32[32,4096]{1,0:T(8,128)}, u32[]{:S(2)}, u32[]{:S(2)}) collective-permute-start(f32[32,4096]{1,0:T(8,128)S(1)} %get-tuple-element.70), channel_id=1, source_target_pairs={{0,8},{4,12},{8,0},{12,4},{16,24},{20,28},{24,16},{28,20},{1,9},{5... | collective-permute-start | bytes 1572872 | tf_op jit(solution)/shard_map/ppermute | solution.py:24
  92.9 1.0 copy-start.4
  107.7 106.9 %reduce-scatter.5.cloned.1.call-start = ((), (), s32[]{:S(2)}) async-start(), calls=%async_computation.3 | async-start | bytes 2129920 | tf_op jit(solution)/shard_map/reduce_scatter | solution.py:83
  107.9 8.2 %copy-start.6 = (bf16[64,4096]{1,0:T(8,128)(2,1)S(1)}, bf16[64,4096]{1,0:T(8,128)(2,1)}, u32[]{:S(2)}) copy-start(bf16[64,4096]{1,0:T(8,128)(2,1)} %param.7) | copy-start | bytes 1572868
  117.8 3.8 %collective-permute-start.20 = (f32[32]{0:T(128)S(1)}, f32[32]{0:T(128)S(1)}, u32[]{:S(2)}, u32[]{:S(2)}) collective-permute-start(f32[32]{0:T(128)S(1)} %get-tuple-element.54), channel_id=1, source_target_pairs={{0,3},{1,0},{2,1},{3,2},{4,7},{5,4},{6,5},{7,6},{8,11},{9,8},{10,9... | collective-permute-start | bytes 392 | tf_op jit(solution)/shard_map/ppermute | solution.py:27
  118.3 4.6 %collective-permute-start.19 = (f32[32]{0:T(128)S(1)}, f32[32]{0:T(128)S(1)}, u32[]{:S(2)}, u32[]{:S(2)}) collective-permute-start(f32[32]{0:T(128)S(1)} %get-tuple-element.54), channel_id=1, source_target_pairs={{0,2},{1,3},{2,0},{3,1},{4,6},{5,7},{6,4},{7,5},{8,10},{9,11},{10,... | collective-permute-start | bytes 392 | tf_op jit(solution)/shard_map/ppermute | solution.py:27
  119.2 5.7 %collective-permute-start.18 = (f32[32]{0:T(128)S(1)}, f32[32]{0:T(128)S(1)}, u32[]{:S(2)}, u32[]{:S(2)}) collective-permute-start(f32[32]{0:T(128)S(1)} %get-tuple-element.54), channel_id=1, source_target_pairs={{0,1},{1,2},{2,3},{3,0},{4,5},{5,6},{6,7},{7,4},{8,9},{9,10},{10,1... | collective-permute-start | bytes 392 | tf_op jit(solution)/shard_map/ppermute | solution.py:27
  125.0 17.6 %collective-permute-start.22 = (bf16[32,4096]{1,0:T(8,128)(2,1)S(1)}, bf16[32,4096]{1,0:T(8,128)(2,1)S(1)}, u32[]{:S(2)}, u32[]{:S(2)}) collective-permute-start(bf16[32,4096]{1,0:T(8,128)(2,1)S(1)} %multiply_convert_fusion), channel_id=1, source_target_pairs={{0,16},{4,20},{8,24},{12,28},{16,0},{20,4},{24,8},{28,12},{1,17},{... | collective-permute-start | bytes 786440 | tf_op jit(solution)/shard_map/ppermute | solution.py:24
  125.4 17.2 %collective-permute-start.21 = (bf16[32,4096]{1,0:T(8,128)(2,1)S(1)}, bf16[32,4096]{1,0:T(8,128)(2,1)S(1)}, u32[]{:S(2)}, u32[]{:S(2)}) collective-permute-start(bf16[32,4096]{1,0:T(8,128)(2,1)S(1)} %multiply_convert_fusion), channel_id=1, source_target_pairs={{0,8},{4,12},{8,0},{12,4},{16,24},{20,28},{24,16},{28,20},{1,9},{5... | collective-permute-start | bytes 786440 | tf_op jit(solution)/shard_map/ppermute | solution.py:24
  126.9 15.7 %collective-permute-start.23 = (bf16[32,4096]{1,0:T(8,128)(2,1)S(1)}, bf16[32,4096]{1,0:T(8,128)(2,1)S(1)}, u32[]{:S(2)}, u32[]{:S(2)}) collective-permute-start(bf16[32,4096]{1,0:T(8,128)(2,1)S(1)} %multiply_convert_fusion), channel_id=1, source_target_pairs={{0,24},{4,28},{8,16},{12,20},{16,8},{20,12},{24,0},{28,4},{1,25},{... | collective-permute-start | bytes 786440 | tf_op jit(solution)/shard_map/ppermute | solution.py:24
  143.0 2.9 %collective-permute-start.24 = (bf16[4,32,4096]{2,1,0:T(8,128)(2,1)S(1)}, bf16[4,32,4096]{2,1,0:T(8,128)(2,1)}, u32[]{:S(2)}, u32[]{:S(2)}) collective-permute-start(bf16[4,32,4096]{2,1,0:T(8,128)(2,1)S(1)} %get-tuple-element.75), channel_id=1, source_target_pairs={{0,4},{4,0},{8,12},{12,8},{16,20},{20,16},{24,28},{28,24},{1,5},{5... | collective-permute-start | bytes 3145736 | tf_op jit(solution)/shard_map/ppermute | solution.py:24
  162.6 1.9 copy-start.3
  162.7 20.8 %collective-permute-start.27 = (bf16[1,2,32,3328]{3,2,1,0:T(8,128)(2,1)S(1)}, bf16[1,2,32,3328]{3,2,1,0:T(8,128)(2,1)S(1)}, u32[]{:S(2)}, u32[]{:S(2)}) collective-permute-start(bf16[1,2,32,3328]{3,2,1,0:T(8,128)(2,1)S(1)} %get-tuple-element.62), channel_id=1, source_target_pairs={{0,1},{3,2},{4,5},{7,6},{8,9},{11,10},{12,13},{15,14},{16,17},{19,... | collective-permute-start | bytes 1277960 | tf_op jit(solution)/shard_map/ppermute | solution.py:31
  177.6 3.3 %copy-start = (f32[256,3328]{1,0:T(8,128)}, f32[256,3328]{1,0:T(8,128)S(1)}, u32[]{:S(2)}) copy-start(f32[256,3328]{1,0:T(8,128)S(1)} %fusion.25) | copy-start | bytes 10223620
  178.7 57.4 %collective-permute-start.31 = (bf16[1,2,32,3328]{3,2,1,0:T(8,128)(2,1)}, bf16[1,2,32,3328]{3,2,1,0:T(8,128)(2,1)}, u32[]{:S(2)}, u32[]{:S(2)}) collective-permute-start(bf16[1,2,32,3328]{3,2,1,0:T(8,128)(2,1)} %get-tuple-element.66), channel_id=1, source_target_pairs={{0,1},{3,2},{4,5},{7,6},{8,9},{11,10},{12,13},{15,14},{16,17},{19,... | collective-permute-start | bytes 1277960 | tf_op jit(solution)/shard_map/ppermute | solution.py:31
  180.9 33.7 %collective-permute-start.26 = (bf16[2,2,32,3328]{3,2,1,0:T(8,128)(2,1)S(1)}, bf16[2,2,32,3328]{3,2,1,0:T(8,128)(2,1)}, u32[]{:S(2)}, u32[]{:S(2)}) collective-permute-start(bf16[2,2,32,3328]{3,2,1,0:T(8,128)(2,1)S(1)} %pad_maximum_fusion.9), channel_id=1, source_target_pairs={{0,1},{3,2},{4,5},{7,6},{8,9},{11,10},{12,13},{15,14},{16,17},{19,... | collective-permute-start | bytes 2555912 | tf_op jit(solution)/shard_map/ppermute | solution.py:31
  183.6 10.6 %collective-permute-start.28 = (bf16[1,2,32,3328]{3,2,1,0:T(8,128)(2,1)S(1)}, bf16[1,2,32,3328]{3,2,1,0:T(8,128)(2,1)}, u32[]{:S(2)}, u32[]{:S(2)}) collective-permute-start(bf16[1,2,32,3328]{3,2,1,0:T(8,128)(2,1)S(1)} %add_convert_fusion.5), channel_id=1, source_target_pairs={{1,2},{2,1},{5,6},{6,5},{9,10},{10,9},{13,14},{14,13},{17,18},{18,... | collective-permute-start | bytes 1277960 | tf_op jit(solution)/shard_map/ppermute | solution.py:31
  186.1 46.7 %collective-permute-start.25 = (bf16[2,2,32,3328]{3,2,1,0:T(8,128)(2,1)}, bf16[2,2,32,3328]{3,2,1,0:T(8,128)(2,1)}, u32[]{:S(2)}, u32[]{:S(2)}) collective-permute-start(bf16[2,2,32,3328]{3,2,1,0:T(8,128)(2,1)} %pad_maximum_fusion.8), channel_id=1, source_target_pairs={{0,1},{3,2},{4,5},{7,6},{8,9},{11,10},{12,13},{15,14},{16,17},{19,... | collective-permute-start | bytes 2555912 | tf_op jit(solution)/shard_map/ppermute | solution.py:31
  214.6 4.2 %copy-start.7 = (bf16[1,2,32,3328]{3,2,1,0:T(8,128)(2,1)S(1)}, bf16[1,2,32,3328]{3,2,1,0:T(8,128)(2,1)}, u32[]{:S(2)}) copy-start(bf16[1,2,32,3328]{3,2,1,0:T(8,128)(2,1)} %reduce-scatter.3.cloned.1.call-done) | copy-start | bytes 1277956
  214.6 4.2 %copy-start.8 = (bf16[1,2,32,3328]{3,2,1,0:T(8,128)(2,1)S(1)}, bf16[1,2,32,3328]{3,2,1,0:T(8,128)(2,1)}, u32[]{:S(2)}) copy-start(bf16[1,2,32,3328]{3,2,1,0:T(8,128)(2,1)} %reduce-scatter.5.cloned.1.call-done) | copy-start | bytes 1277956
  216.4 16.4 %copy-start.1 = (f32[256,3328]{1,0:T(8,128)S(1)}, f32[256,3328]{1,0:T(8,128)}, u32[]{:S(2)}) copy-start(f32[256,3328]{1,0:T(8,128)} %copy-done) | copy-start | bytes 10223620
  216.4 16.4 %collective-permute-start.30 = (bf16[1,2,32,3328]{3,2,1,0:T(8,128)(2,1)S(1)}, bf16[1,2,32,3328]{3,2,1,0:T(8,128)(2,1)S(1)}, u32[]{:S(2)}, u32[]{:S(2)}) collective-permute-start(bf16[1,2,32,3328]{3,2,1,0:T(8,128)(2,1)S(1)} %get-tuple-element.60), channel_id=1, source_target_pairs={{2,3},{1,0},{6,7},{5,4},{10,11},{9,8},{14,15},{13,12},{18,19},{17,... | collective-permute-start | bytes 1277960 | tf_op jit(solution)/shard_map/ppermute | solution.py:31
  218.1 14.7 %collective-permute-start.29 = (bf16[2,2,32,3328]{3,2,1,0:T(8,128)(2,1)S(1)}, bf16[2,2,32,3328]{3,2,1,0:T(8,128)(2,1)S(1)}, u32[]{:S(2)}, u32[]{:S(2)}) collective-permute-start(bf16[2,2,32,3328]{3,2,1,0:T(8,128)(2,1)S(1)} %pad_maximum_fusion.10), channel_id=1, source_target_pairs={{1,2},{2,1},{5,6},{6,5},{9,10},{10,9},{13,14},{14,13},{17,18},{18,... | collective-permute-start | bytes 2555912 | tf_op jit(solution)/shard_map/ppermute | solution.py:31
  234.0 21.2 %collective-permute-start.33 = (bf16[1,2,32,3328]{3,2,1,0:T(8,128)(2,1)S(1)}, bf16[1,2,32,3328]{3,2,1,0:T(8,128)(2,1)S(1)}, u32[]{:S(2)}, u32[]{:S(2)}) collective-permute-start(bf16[1,2,32,3328]{3,2,1,0:T(8,128)(2,1)S(1)} %get-tuple-element.58), channel_id=1, source_target_pairs={{2,3},{1,0},{6,7},{5,4},{10,11},{9,8},{14,15},{13,12},{18,19},{17,... | collective-permute-start | bytes 1277960 | tf_op jit(solution)/shard_map/ppermute | solution.py:31
  235.3 19.9 %collective-permute-start.32 = (bf16[1,2,32,3328]{3,2,1,0:T(8,128)(2,1)S(1)}, bf16[1,2,32,3328]{3,2,1,0:T(8,128)(2,1)S(1)}, u32[]{:S(2)}, u32[]{:S(2)}) collective-permute-start(bf16[1,2,32,3328]{3,2,1,0:T(8,128)(2,1)S(1)} %get-tuple-element.59), channel_id=1, source_target_pairs={{1,2},{2,1},{5,6},{6,5},{9,10},{10,9},{13,14},{14,13},{17,18},{18,... | collective-permute-start | bytes 1277960 | tf_op jit(solution)/shard_map/ppermute | solution.py:31
Sparse Core Ops, SparseCore 0:
  28.0 29.5 all-gather.2
  107.8 34.6 reduce-scatter.2
  145.4 48.5 reduce-scatter.4

commit v2 on v1

v2 whole, which is shorter than its diff:
```python
import jax
import jax.numpy as jnp
from jax import lax
from jax.sharding import PartitionSpec as P

F32, BF16 = jnp.float32, jnp.bfloat16
SHARES = (32, 32)


def pick(value, index, axis=0):
    return lax.dynamic_index_in_dim(value, index, axis, keepdims=False)


def tie(value, after):
    return lax.optimization_barrier((value, after))[0] if after else value


def solution(mesh):
    wide, narrow = mesh.shape["wide"], mesh.shape["narrow"]
    chips = wide // 2
    assert chips == narrow

    def swap(value, bits):
        return lax.ppermute(value, "wide", [(i, i ^ bits) for i in range(wide)])

    def shift(value, by):
        return lax.ppermute(value, "narrow", [(i, (i + by) % narrow) for i in range(narrow)])

    def hop(value, step):
        pairs = [(step - 1, step), (narrow - step, narrow - 1 - step)]
        return lax.ppermute(value, "narrow", pairs)

    def on_device(heads_output, residual_in, out_weight, norm_gain, gate_weight, up_weight):
        me, place = lax.axis_index("wide"), lax.axis_index("narrow")
        chip, core = me // 2, me % 2
        rows, width = residual_in.shape
        features = width * narrow
        depth = heads_output.shape[1]
        heads = heads_output.reshape(2, rows, depth)

        def fetch(at, share, after):
            own = tie(heads[:, at : at + share], after)
            return jnp.stack([own] + [shift(own, s) for s in range(1, narrow)])

        def project(stacked):
            share = stacked.shape[2]

            def terms(which):
                left = pick(stacked, which, 1).reshape(narrow * share, depth)
                return jnp.dot(left, out_weight, preferred_element_type=F32)

            sent = terms(1 - core)
            got = swap(sent, 1)
            kept, _ = lax.optimization_barrier((terms(core), sent))
            return kept, got

        def spread(kept, got, travel):
            total = (kept + got).reshape(narrow, -1, width)

            def for_chip(d):
                return pick(total, (place - (chip ^ d)) % narrow)

            sent = [for_chip(d).astype(travel) for d in range(1, chips)]
            return for_chip(0), sent, [swap(part, 2 * d) for d, part in enumerate(sent, 1)]

        def scale_of(residual, after):
            own = jnp.sum(residual * residual, axis=1)
            others = tie([shift(own, s) for s in range(1, narrow)], after)
            return 1.0 / jnp.sqrt(sum(others, own) / features + 1e-05)

        def gather(normed, after):
            return jnp.stack([normed] + tie([swap(normed, 2 * d) for d in range(1, chips)], after))

        def both(near):
            near = jnp.stack([pick(near, j ^ chip) for j in range(chips)])
            return jnp.stack([near, swap(near, 1)], 1)

        def multiply(all_rows, weight, after):
            left = tie(all_rows.reshape(-1, width), after)
            terms = jnp.dot(left, weight, preferred_element_type=F32)
            return terms.reshape(*all_rows.shape[:-1], -1)

        totals, flying, last = {}, [], ()

        def stage(entering, beside=None, after=()):
            nonlocal flying, last
            lanes = {}
            for terms, b in entering:
                totals.setdefault(id(terms), pick(terms, place))
            for terms, b, step, carried in flying + [(terms, b, 0, 0.0) for terms, b in entering]:
                index = jnp.where(place == step, b, narrow - 1 - b)
                part = (pick(terms, index) + carried).astype(BF16)
                lanes.setdefault(step + 1, []).append((terms, b, part))
            parts = {step: jnp.stack([part for _, _, part in lane]) for step, lane in lanes.items()}
            parts, _ = lax.optimization_barrier((parts, (last, after)))
            moved = {step: hop(part, step) for step, part in parts.items()}
            last = tuple(moved.values())
            product = beside(tuple(parts.values())) if beside else ()
            moved, _ = lax.optimization_barrier((moved, product))
            flying = []
            for step, lane in lanes.items():
                for (terms, b, _), value in zip(lane, moved[step]):
                    if step == b:
                        totals[id(terms)] = totals[id(terms)] + value
                    else:
                        flying.append((terms, b, step, value))
            return product

        first, second = SHARES
        far = narrow - 1
        stacked_a = fetch(0, first, ())
        kept_a, got_a = project(stacked_a)
        stacked_b = fetch(first, second, (stacked_a,))
        own_a, _, parts_a = spread(kept_a, got_a, BF16)
        parts_a = tie(parts_a, (stacked_b,))
        residual_a = residual_in[:first].astype(F32) + sum(parts_a, own_a)
        scale_a = scale_of(residual_a, ())
        normed_a = (residual_a * scale_a[:, None] * norm_gain).astype(BF16)
        kept_b, got_b = project(tie(stacked_b, (normed_a,)))
        near_a = gather(normed_a, (kept_b,))
        rows_a = both(near_a)

        own_b, sent_b, parts_b = spread(tie(kept_b, (near_a,)), got_b, F32)
        gate_a = multiply(rows_a, gate_weight, (sent_b,))
        up_a = stage(
            [(gate_a, b) for b in range(far, 1, -1)],
            lambda sent: multiply(rows_a, up_weight, (gate_a, sent)),
        )
        residual_b = residual_in[first:].astype(F32) + sum(tie(parts_b, (up_a,)), own_b)
        scale_b = scale_of(residual_b, ())
        normed_b = (residual_b * scale_b[:, None] * norm_gain).astype(BF16)
        rows_b = both(
            stage(
                [(gate_a, 1), (up_a, far)],
                lambda sent: gather(tie(normed_b, (sent,)), ()),
                (normed_b,),
            )
        )
        before = last

        def products(sent):
            gate = multiply(rows_b, gate_weight, (before, sent))
            return gate, multiply(rows_b, up_weight, (gate,))

        gate_b, up_b = stage([(up_a, b) for b in range(far - 1, 0, -1)], products)
        for b in range(far, 0, -1):
            stage([(gate_b, b), (up_b, b)])
        while flying:
            stage([])
        gate_sum_a, up_sum_a, gate_sum_b, up_sum_b = (totals[id(t)] for t in (gate_a, up_a, gate_b, up_b))

        residuals = [residual_a, residual_b]
        outs = []
        for gate, up in ((gate_sum_a, up_sum_a), (gate_sum_b, up_sum_b)):
            hidden = jax.nn.silu(gate) * up
            outs.append(jnp.where(core == 0, hidden, hidden[::-1]))
        hidden = jnp.concatenate(outs, axis=1)
        return jnp.concatenate(residuals, axis=0), hidden.reshape(2 * rows, -1)

    in_specs = (
        P("narrow", "wide"),
        P("wide", "narrow"),
        P("wide", "narrow"),
        P("narrow"),
        P("narrow", "wide"),
        P("narrow", "wide"),
    )
    out_specs = (P("wide", "narrow"), P("narrow", "wide"))
    return jax.shard_map(on_device, mesh=mesh, in_specs=in_specs, out_specs=out_specs, check_vma=False)
```

time: 266 us -> 238 us (0.89)
  waiting for transfers between devices: 102 us -> 80.2 us
  starting transfers between devices: 50.4 us -> 66 us
  between operations: 14.4 us -> 1.39 us
  local copies, waits for them, and re-layouts: 9.24 us -> 2.29 us
    all_gather x1 -> x0, waiting for transfers between devices: 18.6 us -> none  [on_device(): whole = lax.all_gather(tie(heads, (stacked_a,)), 'narrow', axis=0)]
    ppermute x9 -> x14, starting transfers between devices: 19.8 us -> 30 us  [hop(): return lax.ppermute(value, 'narrow', pairs)]
    ppermute x9 -> x12, waiting for transfers between devices: 15.3 us -> 22.6 us  [shift(): lax.ppermute(value, 'narrow', [(i, (i + by) % narrow) for i in range(narr...]
    ppermute x9 -> x14, waiting for transfers between devices: 53.7 us -> 46.4 us  [hop(): return lax.ppermute(value, 'narrow', pairs)]
    ppermute x9 -> x12, starting transfers between devices: 15.9 us -> 21.5 us  [shift(): lax.ppermute(value, 'narrow', [(i, (i + by) % narrow) for i in range(narr...]
    ppermute x16, waiting for transfers between devices: 14.7 us -> 11.2 us  [swap(): return lax.ppermute(value, 'wide', [(i, i ^ bits) for i in range(wide)])]
  transfers between devices with their start and end apart: 37 -> 42, of which waited for: 17 -> 19; matrix products, arithmetic and copies ran while one was open for 32% -> 33% of each run, Pallas kernels for 0% -> 0%
where the time goes in v2:
time: 238 us; the launch traced here: 237 us
  waiting for transfers between devices  80.2 us (34%)
  matrix products  68.9 us (29%)
  starting transfers between devices  66 us (28%)
  other arithmetic  18.7 us (8%)
    dot_general x4, matrix products, multiply(): terms = jnp.dot(left, weight, preferred_element_type=F32)  52.1 us
    ppermute x14, waiting for transfers between devices, hop(): return lax.ppermute(value, 'narrow', pairs)  46.4 us
    ppermute x14, starting transfers between devices, hop(): return lax.ppermute(value, 'narrow', pairs)  30 us
    ppermute x12, waiting for transfers between devices, shift(): lax.ppermute(value, 'narrow', [(i, (i + by) % narrow) for i in range(narr...  22.6 us
    ppermute x12, starting transfers between devices, shift(): lax.ppermute(value, 'narrow', [(i, (i + by) % narrow) for i in range(narr...  21.5 us
    dot_general x4, matrix products, terms(): return jnp.dot(left, out_weight, preferred_element_type=F32)  16.8 us
    ppermute x16, starting transfers between devices, swap(): return lax.ppermute(value, 'wide', [(i, i ^ bits) for i in range(wide)])  14.4 us
    ppermute x16, waiting for transfers between devices, swap(): return lax.ppermute(value, 'wide', [(i, i ^ bits) for i in range(wide)])  11.2 us
  transfers between devices with their start and end apart: 42, of which 19 were waited for; matrix products, arithmetic and copies ran while one was open for 33% of the time, Pallas kernels for 0%

profile of v2, /device:TPU:0, one launch (start us, length us, event | category | flops | bytes accessed | tf_op | source)
XLA Modules:
  0.0 237.4 jit_solution(9313141681506745050)
XLA Ops:
  0.6 1.0 slice_bitcast_fusion
  1.6 4.1 %collective-permute-start.1 = (bf16[2,32,1024]{2,1,0:T(8,128)(2,1)S(1)}, bf16[2,32,1024]{2,1,0:T(8,128)(2,1)S(1)}, u32[]{:S(2)}, u32[]{:S(2)}) collective-permute-start(bf16[2,32,1024]{2,1,0:T(8,128)(2,1)S(1)} %get-tuple-element.146), channel_id=1, source_target_pairs={{0,2},{1,3},{2,0},{3,1},{4,6},{5,7},{6,4},{7,5},{8,10},{9,11},{10,... | collective-permute-start | bytes 393224 | tf_op jit(solution)/shard_map/ppermute | solution.py:27
  5.7 1.6 collective-permute-start
  7.3 2.2 collective-permute-start.2
  9.6 6.2 %collective-permute-done.1 = bf16[2,32,1024]{2,1,0:T(8,128)(2,1)S(1)} collective-permute-done((bf16[2,32,1024]{2,1,0:T(8,128)(2,1)S(1)}, bf16[2,32,1024]{2,1,0:T(8,128)(2,1)S(1)}, u32[]{:S(2)}, u32[]{:S(2)}) %collective-permute-start.1) | collective-permute-done | bytes 131104 | tf_op jit(solution)/shard_map/ppermute | solution.py:27
  16.6 4.7 %fusion.20 = f32[128,4096]{1,0:T(8,128)S(1)} fusion(bf16[128,1024]{1,0:T(8,128)(2,1)S(1)} %bitcast.146, bf16[1024,4096]{1,0:T(8,128)(2,1)} %param.8), kind=kOutput, calls=%fused_computation.97 | convolution fusion | flops 1073741824 | bytes 10747904 | tf_op jit(solution)/shard_map/dot_general | solution.py:50
  21.4 2.1 collective-permute-start.9
  23.6 4.7 %fusion.19 = f32[128,4096]{1,0:T(8,128)S(1)} fusion(bf16[128,1024]{1,0:T(8,128)(2,1)S(1)} %bitcast.143, bf16[1024,4096]{1,0:T(8,128)(2,1)} %param.8), kind=kOutput, calls=%fused_computation.96 | convolution fusion | flops 1073741824 | bytes 10747904 | tf_op jit(solution)/shard_map/dot_general | solution.py:50
  28.3 1.9 add.265
  30.3 2.5 %collective-permute-start.6 = (bf16[32,4096]{1,0:T(8,128)(2,1)S(1)}, bf16[32,4096]{1,0:T(8,128)(2,1)}, u32[]{:S(2)}, u32[]{:S(2)}) collective-permute-start(bf16[32,4096]{1,0:T(8,128)(2,1)S(1)} %get-tuple-element.121), channel_id=1, source_target_pairs={{0,24},{4,28},{8,16},{12,20},{16,8},{20,12},{24,0},{28,4},{1,25},{... | collective-permute-start | bytes 786440 | tf_op jit(solution)/shard_map/ppermute | solution.py:24
  33.9 1.8 collective-permute-start.8
  35.7 2.0 collective-permute-start.7
  37.7 7.4 %collective-permute-done.8 = bf16[2,32,1024]{2,1,0:T(8,128)(2,1)} collective-permute-done((bf16[2,32,1024]{2,1,0:T(8,128)(2,1)S(1)}, bf16[2,32,1024]{2,1,0:T(8,128)(2,1)}, u32[]{:S(2)}, u32[]{:S(2)}) %collective-permute-start.8) | collective-permute-done | bytes 131104 | tf_op jit(solution)/shard_map/ppermute | solution.py:27
  45.1 1.1 pad_maximum_fusion.19
  46.3 1.4 multiply_reduce_fusion.1
  47.7 2.4 %collective-permute-start.12 = (f32[32]{0:T(128)S(1)}, f32[32]{0:T(128)S(1)}, u32[]{:S(2)}, u32[]{:S(2)}) collective-permute-start(f32[32]{0:T(128)S(1)} %get-tuple-element.96), channel_id=1, source_target_pairs={{0,3},{1,0},{2,1},{3,2},{4,7},{5,4},{6,5},{7,6},{8,11},{9,8},{10,9... | collective-permute-start | bytes 392 | tf_op jit(solution)/shard_map/ppermute | solution.py:27
  50.1 1.7 collective-permute-start.10
  51.8 2.7 %collective-permute-done.11 = f32[32]{0:T(128)S(1)} collective-permute-done((f32[32]{0:T(128)S(1)}, f32[32]{0:T(128)S(1)}, u32[]{:S(2)}, u32[]{:S(2)}) %collective-permute-start.11) | collective-permute-done | bytes 160 | tf_op jit(solution)/shard_map/ppermute | solution.py:27
  54.5 0.9 collective-permute-done.10
  55.7 1.5 collective-permute-start.14
  57.2 1.4 collective-permute-start.13
  59.3 6.2 %fusion.22 = f32[128,4096]{1,0:T(8,128)} fusion(bf16[128,1024]{1,0:T(8,128)(2,1)S(1)} %bitcast.145, bf16[1024,4096]{1,0:T(8,128)(2,1)} %param.8), kind=kOutput, calls=%fused_computation.99 | convolution fusion | flops 1073741824 | bytes 10747904 | tf_op jit(solution)/shard_map/dot_general | solution.py:50
  65.5 1.3 fusion.21
  66.9 2.4 %collective-permute-done.15 = bf16[32,4096]{1,0:T(8,128)(2,1)S(1)} collective-permute-done((bf16[32,4096]{1,0:T(8,128)(2,1)S(1)}, bf16[32,4096]{1,0:T(8,128)(2,1)S(1)}, u32[]{:S(2)}, u32[]{:S(2)}) %collective-permute-start.15) | collective-permute-done | bytes 262176 | tf_op jit(solution)/shard_map/ppermute | solution.py:24
  69.5 1.5 fusion.16
  71.0 3.0 %collective-permute-done.20 = bf16[4,32,4096]{2,1,0:T(8,128)(2,1)} collective-permute-done((bf16[4,32,4096]{2,1,0:T(8,128)(2,1)}, bf16[4,32,4096]{2,1,0:T(8,128)(2,1)}, u32[]{:S(2)}, u32[]{:S(2)}) %collective-permute-start.20) | collective-permute-done | bytes 1048608 | tf_op jit(solution)/shard_map/ppermute | solution.py:24
  74.0 1.7 pad_maximum_fusion
  75.7 1.8 add.282
  77.7 2.1 collective-permute-start.19
  79.8 0.9 collective-permute-start.18
  81.2 13.0 %fusion.23 = f32[256,3328]{1,0:T(8,128)S(1)} fusion(bf16[256,4096]{1,0:T(8,128)(2,1)S(1)} %bitcast.138, bf16[4096,3328]{1,0:T(8,128)(2,1)} %param.10), kind=kOutput, calls=%fused_computation.100 | convolution fusion | flops 6979321856 | bytes 32768000 | tf_op jit(solution)/shard_map/dot_general | solution.py:80
  94.4 1.5 collective-permute-start.21
  95.9 13.1 %fusion.24 = f32[256,3328]{1,0:T(8,128)S(1)} fusion(bf16[256,4096]{1,0:T(8,128)(2,1)S(1)} %bitcast.139, bf16[4096,3328]{1,0:T(8,128)(2,1)} %param.11), kind=kOutput, calls=%fused_computation.101 | convolution fusion | flops 6979321856 | bytes 32768000 | tf_op jit(solution)/shard_map/dot_general | solution.py:80
  109.6 2.9 %collective-permute-start.24 = (f32[32]{0:T(128)S(1)}, f32[32]{0:T(128)S(1)}, u32[]{:S(2)}, u32[]{:S(2)}) collective-permute-start(f32[32]{0:T(128)S(1)} %get-tuple-element.94), channel_id=1, source_target_pairs={{0,3},{1,0},{2,1},{3,2},{4,7},{5,4},{6,5},{7,6},{8,11},{9,8},{10,9... | collective-permute-start | bytes 392 | tf_op jit(solution)/shard_map/ppermute | solution.py:27
  113.7 3.1 %collective-permute-done.23 = f32[32]{0:T(128)S(1)} collective-permute-done((f32[32]{0:T(128)S(1)}, f32[32]{0:T(128)S(1)}, u32[]{:S(2)}, u32[]{:S(2)}) %collective-permute-start.23) | collective-permute-done | bytes 160 | tf_op jit(solution)/shard_map/ppermute | solution.py:27
  116.9 0.9 collective-permute-done.22
  118.2 1.3 collective-permute-start.29
  119.5 1.7 collective-permute-start.28
  121.7 1.0 pad_maximum_fusion.5
  122.8 1.5 collective-permute-start.25
  124.3 0.7 collective-permute-start.26
  125.0 3.0 %collective-permute-done.29 = bf16[32,4096]{1,0:T(8,128)(2,1)S(1)} collective-permute-done((bf16[32,4096]{1,0:T(8,128)(2,1)S(1)}, bf16[32,4096]{1,0:T(8,128)(2,1)S(1)}, u32[]{:S(2)}, u32[]{:S(2)}) %collective-permute-start.29) | collective-permute-done | bytes 262176 | tf_op jit(solution)/shard_map/ppermute | solution.py:24
  128.0 2.7 %collective-permute-done.28 = bf16[32,4096]{1,0:T(8,128)(2,1)S(1)} collective-permute-done((bf16[32,4096]{1,0:T(8,128)(2,1)S(1)}, bf16[32,4096]{1,0:T(8,128)(2,1)S(1)}, u32[]{:S(2)}, u32[]{:S(2)}) %collective-permute-start.28) | collective-permute-done | bytes 262176 | tf_op jit(solution)/shard_map/ppermute | solution.py:24
  131.2 8.6 %collective-permute-done.25 = bf16[2,2,32,3328]{3,2,1,0:T(8,128)(2,1)S(1)} collective-permute-done((bf16[2,2,32,3328]{3,2,1,0:T(8,128)(2,1)S(1)}, bf16[2,2,32,3328]{3,2,1,0:T(8,128)(2,1)S(1)}, u32[]{:S(2)}, u32[]{:S(2)}) %collective-permute-start.25) | collective-permute-done | bytes 852000 | tf_op jit(solution)/shard_map/ppermute | solution.py:31
  139.8 0.9 add_convert_fusion.9
  140.7 0.8 add_convert_fusion.8
  142.2 1.3 collective-permute-start.32
  143.5 9.4 %collective-permute-start.30 = (bf16[2,2,32,3328]{3,2,1,0:T(8,128)(2,1)S(1)}, bf16[2,2,32,3328]{3,2,1,0:T(8,128)(2,1)S(1)}, u32[]{:S(2)}, u32[]{:S(2)}) collective-permute-start(bf16[2,2,32,3328]{3,2,1,0:T(8,128)(2,1)S(1)} %pad_maximum_fusion.11), channel_id=1, source_target_pairs={{0,1},{3,2},{4,5},{7,6},{8,9},{11,10},{12,13},{15,14},{16,17},{19,... | collective-permute-start | bytes 2555912 | tf_op jit(solution)/shard_map/ppermute | solution.py:31
  153.4 13.0 %fusion.25 = f32[256,3328]{1,0:T(8,128)S(1)} fusion(bf16[256,4096]{1,0:T(8,128)(2,1)S(1)} %bitcast.140, bf16[4096,3328]{1,0:T(8,128)(2,1)} %param.10), kind=kOutput, calls=%fused_computation.102 | convolution fusion | flops 6979321856 | bytes 32768000 | tf_op jit(solution)/shard_map/dot_general | solution.py:80
  166.4 13.1 %fusion.26 = f32[256,3328]{1,0:T(8,128)S(1)} fusion(bf16[256,4096]{1,0:T(8,128)(2,1)S(1)} %bitcast.141, bf16[4096,3328]{1,0:T(8,128)(2,1)} %param.11), kind=kOutput, calls=%fused_computation.103 | convolution fusion | flops 6979321856 | bytes 32768000 | tf_op jit(solution)/shard_map/dot_general | solution.py:80
  180.1 1.3 collective-permute-start.34
  182.2 1.3 collective-permute-start.36
  183.6 8.6 %collective-permute-done.36 = bf16[1,2,32,3328]{3,2,1,0:T(8,128)(2,1)S(1)} collective-permute-done((bf16[1,2,32,3328]{3,2,1,0:T(8,128)(2,1)S(1)}, bf16[1,2,32,3328]{3,2,1,0:T(8,128)(2,1)S(1)}, u32[]{:S(2)}, u32[]{:S(2)}) %collective-permute-start.36) | collective-permute-done | bytes 426016 | tf_op jit(solution)/shard_map/ppermute | solution.py:31
  192.2 3.6 %collective-permute-done.34 = bf16[2,2,32,3328]{3,2,1,0:T(8,128)(2,1)S(1)} collective-permute-done((bf16[2,2,32,3328]{3,2,1,0:T(8,128)(2,1)S(1)}, bf16[2,2,32,3328]{3,2,1,0:T(8,128)(2,1)S(1)}, u32[]{:S(2)}, u32[]{:S(2)}) %collective-permute-start.34) | collective-permute-done | bytes 852000 | tf_op jit(solution)/shard_map/ppermute | solution.py:31
  196.1 4.4 %collective-permute-start.37 = (bf16[2,2,32,3328]{3,2,1,0:T(8,128)(2,1)S(1)}, bf16[2,2,32,3328]{3,2,1,0:T(8,128)(2,1)S(1)}, u32[]{:S(2)}, u32[]{:S(2)}) collective-permute-start(bf16[2,2,32,3328]{3,2,1,0:T(8,128)(2,1)S(1)} %pad_maximum_fusion.14), channel_id=1, source_target_pairs={{0,1},{3,2},{4,5},{7,6},{8,9},{11,10},{12,13},{15,14},{16,17},{19,... | collective-permute-start | bytes 2555912 | tf_op jit(solution)/shard_map/ppermute | solution.py:31
  200.5 0.7 collective-permute-start.38
  201.3 1.6 bitcast_multiply_fusion.2
  202.8 11.8 %collective-permute-done.37 = bf16[2,2,32,3328]{3,2,1,0:T(8,128)(2,1)S(1)} collective-permute-done((bf16[2,2,32,3328]{3,2,1,0:T(8,128)(2,1)S(1)}, bf16[2,2,32,3328]{3,2,1,0:T(8,128)(2,1)S(1)}, u32[]{:S(2)}, u32[]{:S(2)}) %collective-permute-start.37) | collective-permute-done | bytes 852000 | tf_op jit(solution)/shard_map/ppermute | solution.py:31
  215.2 4.5 %collective-permute-start.39 = (bf16[2,2,32,3328]{3,2,1,0:T(8,128)(2,1)S(1)}, bf16[2,2,32,3328]{3,2,1,0:T(8,128)(2,1)S(1)}, u32[]{:S(2)}, u32[]{:S(2)}) collective-permute-start(bf16[2,2,32,3328]{3,2,1,0:T(8,128)(2,1)S(1)} %pad_maximum_fusion.13), channel_id=1, source_target_pairs={{0,1},{3,2},{4,5},{7,6},{8,9},{11,10},{12,13},{15,14},{16,17},{19,... | collective-permute-start | bytes 2555912 | tf_op jit(solution)/shard_map/ppermute | solution.py:31
  219.6 0.7 collective-permute-start.40
  220.4 1.3 collective-permute-start.41
  221.7 10.1 %collective-permute-done.39 = bf16[2,2,32,3328]{3,2,1,0:T(8,128)(2,1)S(1)} collective-permute-done((bf16[2,2,32,3328]{3,2,1,0:T(8,128)(2,1)S(1)}, bf16[2,2,32,3328]{3,2,1,0:T(8,128)(2,1)S(1)}, u32[]{:S(2)}, u32[]{:S(2)}) %collective-permute-start.39) | collective-permute-done | bytes 852000 | tf_op jit(solution)/shard_map/ppermute | solution.py:31
  231.8 3.7 %collective-permute-done.41 = bf16[2,2,32,3328]{3,2,1,0:T(8,128)(2,1)S(1)} collective-permute-done((bf16[2,2,32,3328]{3,2,1,0:T(8,128)(2,1)S(1)}, bf16[2,2,32,3328]{3,2,1,0:T(8,128)(2,1)S(1)}, u32[]{:S(2)}, u32[]{:S(2)}) %collective-permute-start.41) | collective-permute-done | bytes 852000 | tf_op jit(solution)/shard_map/ppermute | solution.py:31
  236.1 1.3 pad_maximum_fusion.2
  (91 shorter events, 11.5 us)
Async XLA Ops:
  1.6 14.1 %collective-permute-start.1 = (bf16[2,32,1024]{2,1,0:T(8,128)(2,1)S(1)}, bf16[2,32,1024]{2,1,0:T(8,128)(2,1)S(1)}, u32[]{:S(2)}, u32[]{:S(2)}) collective-permute-start(bf16[2,32,1024]{2,1,0:T(8,128)(2,1)S(1)} %get-tuple-element.146), channel_id=1, source_target_pairs={{0,2},{1,3},{2,0},{3,1},{4,6},{5,7},{6,4},{7,5},{8,10},{9,11},{10,... | collective-permute-start | bytes 393224 | tf_op jit(solution)/shard_map/ppermute | solution.py:27
  5.7 10.0 %collective-permute-start = (bf16[2,32,1024]{2,1,0:T(8,128)(2,1)S(1)}, bf16[2,32,1024]{2,1,0:T(8,128)(2,1)S(1)}, u32[]{:S(2)}, u32[]{:S(2)}) collective-permute-start(bf16[2,32,1024]{2,1,0:T(8,128)(2,1)S(1)} %get-tuple-element.146), channel_id=1, source_target_pairs={{0,1},{1,2},{2,3},{3,0},{4,5},{5,6},{6,7},{7,4},{8,9},{9,10},{10,1... | collective-permute-start | bytes 393224 | tf_op jit(solution)/shard_map/ppermute | solution.py:27
  7.3 9.1 %collective-permute-start.2 = (bf16[2,32,1024]{2,1,0:T(8,128)(2,1)S(1)}, bf16[2,32,1024]{2,1,0:T(8,128)(2,1)S(1)}, u32[]{:S(2)}, u32[]{:S(2)}) collective-permute-start(bf16[2,32,1024]{2,1,0:T(8,128)(2,1)S(1)} %get-tuple-element.146), channel_id=1, source_target_pairs={{0,3},{1,0},{2,1},{3,2},{4,7},{5,4},{6,5},{7,6},{8,11},{9,8},{10,9... | collective-permute-start | bytes 393224 | tf_op jit(solution)/shard_map/ppermute | solution.py:27
  21.3 7.0 %collective-permute-start.3 = (f32[128,4096]{1,0:T(8,128)S(1)}, f32[128,4096]{1,0:T(8,128)}, u32[]{:S(2)}, u32[]{:S(2)}) collective-permute-start(f32[128,4096]{1,0:T(8,128)S(1)} %fusion.20), channel_id=1, source_target_pairs={{0,4},{4,0},{8,12},{12,8},{16,20},{20,16},{24,28},{28,24},{1,5},{5... | collective-permute-start | bytes 6291464 | tf_op jit(solution)/shard_map/ppermute | solution.py:24
  21.4 14.3 %collective-permute-start.9 = (bf16[2,32,1024]{2,1,0:T(8,128)(2,1)S(1)}, bf16[2,32,1024]{2,1,0:T(8,128)(2,1)}, u32[]{:S(2)}, u32[]{:S(2)}) collective-permute-start(bf16[2,32,1024]{2,1,0:T(8,128)(2,1)S(1)} %get-tuple-element.49), channel_id=1, source_target_pairs={{0,3},{1,0},{2,1},{3,2},{4,7},{5,4},{6,5},{7,6},{8,11},{9,8},{10,9... | collective-permute-start | bytes 393224 | tf_op jit(solution)/shard_map/ppermute | solution.py:27
  28.2 18.0 %copy-start.2 = (bf16[64,4096]{1,0:T(8,128)(2,1)S(1)}, bf16[64,4096]{1,0:T(8,128)(2,1)}, u32[]{:S(2)}) copy-start(bf16[64,4096]{1,0:T(8,128)(2,1)} %param.7) | copy-start | bytes 1572868
  30.2 25.2 %copy-start.3 = (f32[4096]{0:T(1024)S(1)}, f32[4096]{0:T(1024)}, u32[]{:S(2)}) copy-start(f32[4096]{0:T(1024)} %param.9) | copy-start | bytes 49156
  30.3 15.9 %collective-permute-start.6 = (bf16[32,4096]{1,0:T(8,128)(2,1)S(1)}, bf16[32,4096]{1,0:T(8,128)(2,1)}, u32[]{:S(2)}, u32[]{:S(2)}) collective-permute-start(bf16[32,4096]{1,0:T(8,128)(2,1)S(1)} %get-tuple-element.121), channel_id=1, source_target_pairs={{0,24},{4,28},{8,16},{12,20},{16,8},{20,12},{24,0},{28,4},{1,25},{... | collective-permute-start | bytes 786440 | tf_op jit(solution)/shard_map/ppermute | solution.py:24
  32.8 13.4 %collective-permute-start.5 = (bf16[32,4096]{1,0:T(8,128)(2,1)S(1)}, bf16[32,4096]{1,0:T(8,128)(2,1)}, u32[]{:S(2)}, u32[]{:S(2)}) collective-permute-start(bf16[32,4096]{1,0:T(8,128)(2,1)S(1)} %get-tuple-element.122), channel_id=1, source_target_pairs={{0,16},{4,20},{8,24},{12,28},{16,0},{20,4},{24,8},{28,12},{1,17},{... | collective-permute-start | bytes 786440 | tf_op jit(solution)/shard_map/ppermute | solution.py:24
  33.3 12.9 %collective-permute-start.4 = (bf16[32,4096]{1,0:T(8,128)(2,1)S(1)}, bf16[32,4096]{1,0:T(8,128)(2,1)}, u32[]{:S(2)}, u32[]{:S(2)}) collective-permute-start(bf16[32,4096]{1,0:T(8,128)(2,1)S(1)} %get-tuple-element.123), channel_id=1, source_target_pairs={{0,8},{4,12},{8,0},{12,4},{16,24},{20,28},{24,16},{28,20},{1,9},{5... | collective-permute-start | bytes 786440 | tf_op jit(solution)/shard_map/ppermute | solution.py:24
  33.9 11.2 %collective-permute-start.8 = (bf16[2,32,1024]{2,1,0:T(8,128)(2,1)S(1)}, bf16[2,32,1024]{2,1,0:T(8,128)(2,1)}, u32[]{:S(2)}, u32[]{:S(2)}) collective-permute-start(bf16[2,32,1024]{2,1,0:T(8,128)(2,1)S(1)} %get-tuple-element.49), channel_id=1, source_target_pairs={{0,2},{1,3},{2,0},{3,1},{4,6},{5,7},{6,4},{7,5},{8,10},{9,11},{10,... | collective-permute-start | bytes 393224 | tf_op jit(solution)/shard_map/ppermute | solution.py:27
  35.7 9.4 %collective-permute-start.7 = (bf16[2,32,1024]{2,1,0:T(8,128)(2,1)S(1)}, bf16[2,32,1024]{2,1,0:T(8,128)(2,1)}, u32[]{:S(2)}, u32[]{:S(2)}) collective-permute-start(bf16[2,32,1024]{2,1,0:T(8,128)(2,1)S(1)} %get-tuple-element.49), channel_id=1, source_target_pairs={{0,1},{1,2},{2,3},{3,0},{4,5},{5,6},{6,7},{7,4},{8,9},{9,10},{10,1... | collective-permute-start | bytes 393224 | tf_op jit(solution)/shard_map/ppermute | solution.py:27
  47.7 4.2 %collective-permute-start.12 = (f32[32]{0:T(128)S(1)}, f32[32]{0:T(128)S(1)}, u32[]{:S(2)}, u32[]{:S(2)}) collective-permute-start(f32[32]{0:T(128)S(1)} %get-tuple-element.96), channel_id=1, source_target_pairs={{0,3},{1,0},{2,1},{3,2},{4,7},{5,4},{6,5},{7,6},{8,11},{9,8},{10,9... | collective-permute-start | bytes 392 | tf_op jit(solution)/shard_map/ppermute | solution.py:27
  50.1 4.4 %collective-permute-start.11 = (f32[32]{0:T(128)S(1)}, f32[32]{0:T(128)S(1)}, u32[]{:S(2)}, u32[]{:S(2)}) collective-permute-start(f32[32]{0:T(128)S(1)} %get-tuple-element.96), channel_id=1, source_target_pairs={{0,2},{1,3},{2,0},{3,1},{4,6},{5,7},{6,4},{7,5},{8,10},{9,11},{10,... | collective-permute-start | bytes 392 | tf_op jit(solution)/shard_map/ppermute | solution.py:27
  50.1 5.3 %collective-permute-start.10 = (f32[32]{0:T(128)S(1)}, f32[32]{0:T(128)S(1)}, u32[]{:S(2)}, u32[]{:S(2)}) collective-permute-start(f32[32]{0:T(128)S(1)} %get-tuple-element.96), channel_id=1, source_target_pairs={{0,1},{1,2},{2,3},{3,0},{4,5},{5,6},{6,7},{7,4},{8,9},{9,10},{10,1... | collective-permute-start | bytes 392 | tf_op jit(solution)/shard_map/ppermute | solution.py:27
  55.7 11.2 %collective-permute-start.14 = (bf16[32,4096]{1,0:T(8,128)(2,1)S(1)}, bf16[32,4096]{1,0:T(8,128)(2,1)S(1)}, u32[]{:S(2)}, u32[]{:S(2)}) collective-permute-start(bf16[32,4096]{1,0:T(8,128)(2,1)S(1)} %multiply_convert_fusion.1), channel_id=1, source_target_pairs={{0,16},{4,20},{8,24},{12,28},{16,0},{20,4},{24,8},{28,12},{1,17},{... | collective-permute-start | bytes 786440 | tf_op jit(solution)/shard_map/ppermute | solution.py:24
  57.2 9.7 %collective-permute-start.13 = (bf16[32,4096]{1,0:T(8,128)(2,1)S(1)}, bf16[32,4096]{1,0:T(8,128)(2,1)S(1)}, u32[]{:S(2)}, u32[]{:S(2)}) collective-permute-start(bf16[32,4096]{1,0:T(8,128)(2,1)S(1)} %multiply_convert_fusion.1), channel_id=1, source_target_pairs={{0,8},{4,12},{8,0},{12,4},{16,24},{20,28},{24,16},{28,20},{1,9},{5... | collective-permute-start | bytes 786440 | tf_op jit(solution)/shard_map/ppermute | solution.py:24
  58.5 10.7 %collective-permute-start.15 = (bf16[32,4096]{1,0:T(8,128)(2,1)S(1)}, bf16[32,4096]{1,0:T(8,128)(2,1)S(1)}, u32[]{:S(2)}, u32[]{:S(2)}) collective-permute-start(bf16[32,4096]{1,0:T(8,128)(2,1)S(1)} %multiply_convert_fusion.1), channel_id=1, source_target_pairs={{0,24},{4,28},{8,16},{12,20},{16,8},{20,12},{24,0},{28,4},{1,25},{... | collective-permute-start | bytes 786440 | tf_op jit(solution)/shard_map/ppermute | solution.py:24
  59.2 6.2 %slice-start = ((s8[8388608]{0:T(1024)(128)(4,1)}), s8[4194304]{0:T(1024)(128)(4,1)S(1)}, s32[]{:S(2)}) async-start(s8[8388608]{0:T(1024)(128)(4,1)} %bitcast.116), calls=%async_computation | async-start | bytes 8388608
  59.3 6.2 %slice-start.1 = ((s8[8388608]{0:T(1024)(128)(4,1)}), s8[4194304]{0:T(1024)(128)(4,1)S(1)}, s32[]{:S(2)}) async-start(s8[8388608]{0:T(1024)(128)(4,1)} %bitcast.116), calls=%async_computation.1 | async-start | bytes 8388608
  66.8 9.0 %collective-permute-start.16 = (f32[128,4096]{1,0:T(8,128)}, f32[128,4096]{1,0:T(8,128)}, u32[]{:S(2)}, u32[]{:S(2)}) collective-permute-start(f32[128,4096]{1,0:T(8,128)} %fusion.22), channel_id=1, source_target_pairs={{0,4},{4,0},{8,12},{12,8},{16,20},{20,16},{24,28},{28,24},{1,5},{5... | collective-permute-start | bytes 6291464 | tf_op jit(solution)/shard_map/ppermute | solution.py:24
  71.0 3.0 %collective-permute-start.20 = (bf16[4,32,4096]{2,1,0:T(8,128)(2,1)}, bf16[4,32,4096]{2,1,0:T(8,128)(2,1)}, u32[]{:S(2)}, u32[]{:S(2)}) collective-permute-start(bf16[4,32,4096]{2,1,0:T(8,128)(2,1)} %get-tuple-element.133), channel_id=1, source_target_pairs={{0,4},{4,0},{8,12},{12,8},{16,20},{20,16},{24,28},{28,24},{1,5},{5... | collective-permute-start | bytes 3145736 | tf_op jit(solution)/shard_map/ppermute | solution.py:24
  77.7 31.6 %collective-permute-start.19 = (f32[32,4096]{1,0:T(8,128)S(1)}, f32[32,4096]{1,0:T(8,128)S(1)}, u32[]{:S(2)}, u32[]{:S(2)}) collective-permute-start(f32[32,4096]{1,0:T(8,128)S(1)} %get-tuple-element.118), channel_id=1, source_target_pairs={{0,24},{4,28},{8,16},{12,20},{16,8},{20,12},{24,0},{28,4},{1,25},{... | collective-permute-start | bytes 1572872 | tf_op jit(solution)/shard_map/ppermute | solution.py:24
  79.8 29.5 %collective-permute-start.18 = (f32[32,4096]{1,0:T(8,128)S(1)}, f32[32,4096]{1,0:T(8,128)S(1)}, u32[]{:S(2)}, u32[]{:S(2)}) collective-permute-start(f32[32,4096]{1,0:T(8,128)S(1)} %get-tuple-element.119), channel_id=1, source_target_pairs={{0,16},{4,20},{8,24},{12,28},{16,0},{20,4},{24,8},{28,12},{1,17},{... | collective-permute-start | bytes 1572872 | tf_op jit(solution)/shard_map/ppermute | solution.py:24
  80.7 28.6 %collective-permute-start.17 = (f32[32,4096]{1,0:T(8,128)S(1)}, f32[32,4096]{1,0:T(8,128)S(1)}, u32[]{:S(2)}, u32[]{:S(2)}) collective-permute-start(f32[32,4096]{1,0:T(8,128)S(1)} %get-tuple-element.120), channel_id=1, source_target_pairs={{0,8},{4,12},{8,0},{12,4},{16,24},{20,28},{24,16},{28,20},{1,9},{5... | collective-permute-start | bytes 1572872 | tf_op jit(solution)/shard_map/ppermute | solution.py:24
  94.4 23.5 %collective-permute-start.21 = (bf16[2,2,32,3328]{3,2,1,0:T(8,128)(2,1)S(1)}, bf16[2,2,32,3328]{3,2,1,0:T(8,128)(2,1)S(1)}, u32[]{:S(2)}, u32[]{:S(2)}) collective-permute-start(bf16[2,2,32,3328]{3,2,1,0:T(8,128)(2,1)S(1)} %pad_maximum_fusion.8), channel_id=1, source_target_pairs={{0,1},{3,2},{4,5},{7,6},{8,9},{11,10},{12,13},{15,14},{16,17},{19,... | collective-permute-start | bytes 2555912 | tf_op jit(solution)/shard_map/ppermute | solution.py:31
  109.6 4.1 %collective-permute-start.24 = (f32[32]{0:T(128)S(1)}, f32[32]{0:T(128)S(1)}, u32[]{:S(2)}, u32[]{:S(2)}) collective-permute-start(f32[32]{0:T(128)S(1)} %get-tuple-element.94), channel_id=1, source_target_pairs={{0,3},{1,0},{2,1},{3,2},{4,7},{5,4},{6,5},{7,6},{8,11},{9,8},{10,9... | collective-permute-start | bytes 392 | tf_op jit(solution)/shard_map/ppermute | solution.py:27
  112.5 4.4 %collective-permute-start.23 = (f32[32]{0:T(128)S(1)}, f32[32]{0:T(128)S(1)}, u32[]{:S(2)}, u32[]{:S(2)}) collective-permute-start(f32[32]{0:T(128)S(1)} %get-tuple-element.94), channel_id=1, source_target_pairs={{0,2},{1,3},{2,0},{3,1},{4,6},{5,7},{6,4},{7,5},{8,10},{9,11},{10,... | collective-permute-start | bytes 392 | tf_op jit(solution)/shard_map/ppermute | solution.py:27
  112.5 5.3 %collective-permute-start.22 = (f32[32]{0:T(128)S(1)}, f32[32]{0:T(128)S(1)}, u32[]{:S(2)}, u32[]{:S(2)}) collective-permute-start(f32[32]{0:T(128)S(1)} %get-tuple-element.94), channel_id=1, source_target_pairs={{0,1},{1,2},{2,3},{3,0},{4,5},{5,6},{6,7},{7,4},{8,9},{9,10},{10,1... | collective-permute-start | bytes 392 | tf_op jit(solution)/shard_map/ppermute | solution.py:27
  118.2 9.8 %collective-permute-start.29 = (bf16[32,4096]{1,0:T(8,128)(2,1)S(1)}, bf16[32,4096]{1,0:T(8,128)(2,1)S(1)}, u32[]{:S(2)}, u32[]{:S(2)}) collective-permute-start(bf16[32,4096]{1,0:T(8,128)(2,1)S(1)} %multiply_convert_fusion), channel_id=1, source_target_pairs={{0,24},{4,28},{8,16},{12,20},{16,8},{20,12},{24,0},{28,4},{1,25},{... | collective-permute-start | bytes 786440 | tf_op jit(solution)/shard_map/ppermute | solution.py:24
  119.5 11.1 %collective-permute-start.28 = (bf16[32,4096]{1,0:T(8,128)(2,1)S(1)}, bf16[32,4096]{1,0:T(8,128)(2,1)S(1)}, u32[]{:S(2)}, u32[]{:S(2)}) collective-permute-start(bf16[32,4096]{1,0:T(8,128)(2,1)S(1)} %multiply_convert_fusion), channel_id=1, source_target_pairs={{0,16},{4,20},{8,24},{12,28},{16,0},{20,4},{24,8},{28,12},{1,17},{... | collective-permute-start | bytes 786440 | tf_op jit(solution)/shard_map/ppermute | solution.py:24
  121.2 9.5 %collective-permute-start.27 = (bf16[32,4096]{1,0:T(8,128)(2,1)S(1)}, bf16[32,4096]{1,0:T(8,128)(2,1)S(1)}, u32[]{:S(2)}, u32[]{:S(2)}) collective-permute-start(bf16[32,4096]{1,0:T(8,128)(2,1)S(1)} %multiply_convert_fusion), channel_id=1, source_target_pairs={{0,8},{4,12},{8,0},{12,4},{16,24},{20,28},{24,16},{28,20},{1,9},{5... | collective-permute-start | bytes 786440 | tf_op jit(solution)/shard_map/ppermute | solution.py:24
  122.8 17.0 %collective-permute-start.25 = (bf16[2,2,32,3328]{3,2,1,0:T(8,128)(2,1)S(1)}, bf16[2,2,32,3328]{3,2,1,0:T(8,128)(2,1)S(1)}, u32[]{:S(2)}, u32[]{:S(2)}) collective-permute-start(bf16[2,2,32,3328]{3,2,1,0:T(8,128)(2,1)S(1)} %pad_maximum_fusion.9), channel_id=1, source_target_pairs={{0,1},{3,2},{4,5},{7,6},{8,9},{11,10},{12,13},{15,14},{16,17},{19,... | collective-permute-start | bytes 2555912 | tf_op jit(solution)/shard_map/ppermute | solution.py:31
  124.3 15.5 %collective-permute-start.26 = (bf16[2,2,32,3328]{3,2,1,0:T(8,128)(2,1)S(1)}, bf16[2,2,32,3328]{3,2,1,0:T(8,128)(2,1)S(1)}, u32[]{:S(2)}, u32[]{:S(2)}) collective-permute-start(bf16[2,2,32,3328]{3,2,1,0:T(8,128)(2,1)S(1)} %pad_maximum_fusion.10), channel_id=1, source_target_pairs={{1,2},{2,1},{5,6},{6,5},{9,10},{10,9},{13,14},{14,13},{17,18},{18,... | collective-permute-start | bytes 2555912 | tf_op jit(solution)/shard_map/ppermute | solution.py:31
  131.2 21.8 %collective-permute-start.33 = (bf16[4,32,4096]{2,1,0:T(8,128)(2,1)S(1)}, bf16[4,32,4096]{2,1,0:T(8,128)(2,1)S(1)}, u32[]{:S(2)}, u32[]{:S(2)}) collective-permute-start(bf16[4,32,4096]{2,1,0:T(8,128)(2,1)S(1)} %get-tuple-element.127), channel_id=1, source_target_pairs={{0,4},{4,0},{8,12},{12,8},{16,20},{20,16},{24,28},{28,24},{1,5},{5... | collective-permute-start | bytes 3145736 | tf_op jit(solution)/shard_map/ppermute | solution.py:24
  139.8 13.4 %copy-start = (bf16[2,2,32,3328]{3,2,1,0:T(8,128)(2,1)}, bf16[2,2,32,3328]{3,2,1,0:T(8,128)(2,1)S(1)}, u32[]{:S(2)}) copy-start(bf16[2,2,32,3328]{3,2,1,0:T(8,128)(2,1)S(1)} %collective-permute-done.26) | copy-start | bytes 2555908
  141.6 38.3 %collective-permute-start.31 = (bf16[1,2,32,3328]{3,2,1,0:T(8,128)(2,1)}, bf16[1,2,32,3328]{3,2,1,0:T(8,128)(2,1)S(1)}, u32[]{:S(2)}, u32[]{:S(2)}) collective-permute-start(bf16[1,2,32,3328]{3,2,1,0:T(8,128)(2,1)} %add_convert_fusion.9), channel_id=1, source_target_pairs={{1,2},{2,1},{5,6},{6,5},{9,10},{10,9},{13,14},{14,13},{17,18},{18,... | collective-permute-start | bytes 1277960 | tf_op jit(solution)/shard_map/ppermute | solution.py:31
  142.2 37.6 %collective-permute-start.32 = (bf16[1,2,32,3328]{3,2,1,0:T(8,128)(2,1)}, bf16[1,2,32,3328]{3,2,1,0:T(8,128)(2,1)}, u32[]{:S(2)}, u32[]{:S(2)}) collective-permute-start(bf16[1,2,32,3328]{3,2,1,0:T(8,128)(2,1)} %add_convert_fusion.8), channel_id=1, source_target_pairs={{2,3},{1,0},{6,7},{5,4},{10,11},{9,8},{14,15},{13,12},{18,19},{17,... | collective-permute-start | bytes 1277960 | tf_op jit(solution)/shard_map/ppermute | solution.py:31
  143.5 36.3 %collective-permute-start.30 = (bf16[2,2,32,3328]{3,2,1,0:T(8,128)(2,1)S(1)}, bf16[2,2,32,3328]{3,2,1,0:T(8,128)(2,1)S(1)}, u32[]{:S(2)}, u32[]{:S(2)}) collective-permute-start(bf16[2,2,32,3328]{3,2,1,0:T(8,128)(2,1)S(1)} %pad_maximum_fusion.11), channel_id=1, source_target_pairs={{0,1},{3,2},{4,5},{7,6},{8,9},{11,10},{12,13},{15,14},{16,17},{19,... | collective-permute-start | bytes 2555912 | tf_op jit(solution)/shard_map/ppermute | solution.py:31
  180.1 15.8 %collective-permute-start.34 = (bf16[2,2,32,3328]{3,2,1,0:T(8,128)(2,1)S(1)}, bf16[2,2,32,3328]{3,2,1,0:T(8,128)(2,1)S(1)}, u32[]{:S(2)}, u32[]{:S(2)}) collective-permute-start(bf16[2,2,32,3328]{3,2,1,0:T(8,128)(2,1)S(1)} %pad_maximum_fusion.12), channel_id=1, source_target_pairs={{0,1},{3,2},{4,5},{7,6},{8,9},{11,10},{12,13},{15,14},{16,17},{19,... | collective-permute-start | bytes 2555912 | tf_op jit(solution)/shard_map/ppermute | solution.py:31
  181.5 2.1 collective-permute-start.35
  182.2 10.0 %collective-permute-start.36 = (bf16[1,2,32,3328]{3,2,1,0:T(8,128)(2,1)S(1)}, bf16[1,2,32,3328]{3,2,1,0:T(8,128)(2,1)S(1)}, u32[]{:S(2)}, u32[]{:S(2)}) collective-permute-start(bf16[1,2,32,3328]{3,2,1,0:T(8,128)(2,1)S(1)} %get-tuple-element.80), channel_id=1, source_target_pairs={{2,3},{1,0},{6,7},{5,4},{10,11},{9,8},{14,15},{13,12},{18,19},{17,... | collective-permute-start | bytes 1277960 | tf_op jit(solution)/shard_map/ppermute | solution.py:31
  183.5 17.8 %copy-start.1 = (bf16[2,2,32,3328]{3,2,1,0:T(8,128)(2,1)S(1)}, bf16[2,2,32,3328]{3,2,1,0:T(8,128)(2,1)}, u32[]{:S(2)}) copy-start(bf16[2,2,32,3328]{3,2,1,0:T(8,128)(2,1)} %copy-done) | copy-start | bytes 2555908
  196.1 18.6 %collective-permute-start.37 = (bf16[2,2,32,3328]{3,2,1,0:T(8,128)(2,1)S(1)}, bf16[2,2,32,3328]{3,2,1,0:T(8,128)(2,1)S(1)}, u32[]{:S(2)}, u32[]{:S(2)}) collective-permute-start(bf16[2,2,32,3328]{3,2,1,0:T(8,128)(2,1)S(1)} %pad_maximum_fusion.14), channel_id=1, source_target_pairs={{0,1},{3,2},{4,5},{7,6},{8,9},{11,10},{12,13},{15,14},{16,17},{19,... | collective-permute-start | bytes 2555912 | tf_op jit(solution)/shard_map/ppermute | solution.py:31
  200.5 14.1 %collective-permute-start.38 = (bf16[2,2,32,3328]{3,2,1,0:T(8,128)(2,1)S(1)}, bf16[2,2,32,3328]{3,2,1,0:T(8,128)(2,1)S(1)}, u32[]{:S(2)}, u32[]{:S(2)}) collective-permute-start(bf16[2,2,32,3328]{3,2,1,0:T(8,128)(2,1)S(1)} %pad_maximum_fusion.15), channel_id=1, source_target_pairs={{1,2},{2,1},{5,6},{6,5},{9,10},{10,9},{13,14},{14,13},{17,18},{18,... | collective-permute-start | bytes 2555912 | tf_op jit(solution)/shard_map/ppermute | solution.py:31
  215.2 16.6 %collective-permute-start.39 = (bf16[2,2,32,3328]{3,2,1,0:T(8,128)(2,1)S(1)}, bf16[2,2,32,3328]{3,2,1,0:T(8,128)(2,1)S(1)}, u32[]{:S(2)}, u32[]{:S(2)}) collective-permute-start(bf16[2,2,32,3328]{3,2,1,0:T(8,128)(2,1)S(1)} %pad_maximum_fusion.13), channel_id=1, source_target_pairs={{0,1},{3,2},{4,5},{7,6},{8,9},{11,10},{12,13},{15,14},{16,17},{19,... | collective-permute-start | bytes 2555912 | tf_op jit(solution)/shard_map/ppermute | solution.py:31
  219.6 12.2 %collective-permute-start.40 = (bf16[2,2,32,3328]{3,2,1,0:T(8,128)(2,1)S(1)}, bf16[2,2,32,3328]{3,2,1,0:T(8,128)(2,1)S(1)}, u32[]{:S(2)}, u32[]{:S(2)}) collective-permute-start(bf16[2,2,32,3328]{3,2,1,0:T(8,128)(2,1)S(1)} %pad_maximum_fusion.16), channel_id=1, source_target_pairs={{1,2},{2,1},{5,6},{6,5},{9,10},{10,9},{13,14},{14,13},{17,18},{18,... | collective-permute-start | bytes 2555912 | tf_op jit(solution)/shard_map/ppermute | solution.py:31
  220.4 15.1 %collective-permute-start.41 = (bf16[2,2,32,3328]{3,2,1,0:T(8,128)(2,1)S(1)}, bf16[2,2,32,3328]{3,2,1,0:T(8,128)(2,1)S(1)}, u32[]{:S(2)}, u32[]{:S(2)}) collective-permute-start(bf16[2,2,32,3328]{3,2,1,0:T(8,128)(2,1)S(1)} %pad_maximum_fusion.17), channel_id=1, source_target_pairs={{2,3},{1,0},{6,7},{5,4},{10,11},{9,8},{14,15},{13,12},{18,19},{17,... | collective-permute-start | bytes 2555912 | tf_op jit(solution)/shard_map/ppermute | solution.py:31

commit v3 on v2

--- a/solution.py
+++ b/solution.py
@@ -149,13 +149,13 @@
             stage([])
         gate_sum_a, up_sum_a, gate_sum_b, up_sum_b = (totals[id(t)] for t in (gate_a, up_a, gate_b, up_b))
 
-        residuals = [residual_a, residual_b]
-        outs = []
-        for gate, up in ((gate_sum_a, up_sum_a), (gate_sum_b, up_sum_b)):
-            hidden = jax.nn.silu(gate) * up
-            outs.append(jnp.where(core == 0, hidden, hidden[::-1]))
-        hidden = jnp.concatenate(outs, axis=1)
-        return jnp.concatenate(residuals, axis=0), hidden.reshape(2 * rows, -1)
+        hidden = jnp.zeros((2, rows, gate_weight.shape[1]), F32)
+        for at, gate, up in ((0, gate_sum_a, up_sum_a), (first, gate_sum_b, up_sum_b)):
+            part = jax.nn.silu(gate) * up
+            part = jnp.where(core == 0, part, part[::-1])
+            hidden = lax.optimization_barrier(lax.dynamic_update_slice_in_dim(hidden, part, at, 1))
+        residual = jnp.concatenate([residual_a, residual_b], axis=0)
+        return residual, hidden.reshape(2 * rows, -1)
 
     in_specs = (
         P("narrow", "wide"),

time: 238 us -> 238 us (level)
  starting transfers between devices: 66 us -> 62.8 us
  waiting for transfers between devices: 80.2 us -> 83.2 us
    ppermute x12, waiting for transfers between devices: 22.6 us -> 26.8 us  [shift(): lax.ppermute(value, 'narrow', [(i, (i + by) % narrow) for i in range(narr...]
    ppermute x12, starting transfers between devices: 21.5 us -> 17.9 us  [shift(): lax.ppermute(value, 'narrow', [(i, (i + by) % narrow) for i in range(narr...]
  transfers between devices with their start and end apart: 42 -> 42, of which waited for: 19 -> 20; matrix products, arithmetic and copies ran while one was open for 33% -> 32% of each run, Pallas kernels for 0% -> 0%
where the time goes in v3:
time: 238 us
  waiting for transfers between devices  83.2 us (35%)
  matrix products  68.9 us (29%)
  starting transfers between devices  62.8 us (26%)
  other arithmetic  16.7 us (7%)
  local copies, waits for them, and re-layouts  4.57 us (2%)
    dot_general x4, matrix products, multiply(): terms = jnp.dot(left, weight, preferred_element_type=F32)  52.1 us
    ppermute x14, waiting for transfers between devices, hop(): return lax.ppermute(value, 'narrow', pairs)  46.3 us
    ppermute x14, starting transfers between devices, hop(): return lax.ppermute(value, 'narrow', pairs)  30.6 us
    ppermute x12, waiting for transfers between devices, shift(): lax.ppermute(value, 'narrow', [(i, (i + by) % narrow) for i in range(narr...  26.8 us
    ppermute x12, starting transfers between devices, shift(): lax.ppermute(value, 'narrow', [(i, (i + by) % narrow) for i in range(narr...  17.9 us
    dot_general x4, matrix products, terms(): return jnp.dot(left, out_weight, preferred_element_type=F32)  16.8 us
    ppermute x16, starting transfers between devices, swap(): return lax.ppermute(value, 'wide', [(i, i ^ bits) for i in range(wide)])  14.4 us
    ppermute x16, waiting for transfers between devices, swap(): return lax.ppermute(value, 'wide', [(i, i ^ bits) for i in range(wide)])  10.1 us
  transfers between devices with their start and end apart: 42, of which 20 were waited for; matrix products, arithmetic and copies ran while one was open for 32% of the time, Pallas kernels for 0%

profile of v3, /device:TPU:0, one launch (start us, length us, event | category | flops | bytes accessed | tf_op | source)
XLA Modules:
  0.0 237.5 jit_solution(9299801552422303447)
XLA Ops:
  0.6 1.0 slice_bitcast_fusion
  1.6 5.1 %collective-permute-start.2 = (bf16[2,32,1024]{2,1,0:T(8,128)(2,1)S(1)}, bf16[2,32,1024]{2,1,0:T(8,128)(2,1)S(1)}, u32[]{:S(2)}, u32[]{:S(2)}) collective-permute-start(bf16[2,32,1024]{2,1,0:T(8,128)(2,1)S(1)} %get-tuple-element.146), channel_id=1, source_target_pairs={{0,3},{1,0},{2,1},{3,2},{4,7},{5,4},{6,5},{7,6},{8,11},{9,8},{10,9... | collective-permute-start | bytes 393224 | tf_op jit(solution)/shard_map/ppermute | solution.py:27
  6.8 1.0 collective-permute-start
  7.8 2.9 %collective-permute-done.2 = bf16[2,32,1024]{2,1,0:T(8,128)(2,1)S(1)} collective-permute-done((bf16[2,32,1024]{2,1,0:T(8,128)(2,1)S(1)}, bf16[2,32,1024]{2,1,0:T(8,128)(2,1)S(1)}, u32[]{:S(2)}, u32[]{:S(2)}) %collective-permute-start.2) | collective-permute-done | bytes 131104 | tf_op jit(solution)/shard_map/ppermute | solution.py:27
  10.7 7.3 %collective-permute-done.1 = bf16[2,32,1024]{2,1,0:T(8,128)(2,1)S(1)} collective-permute-done((bf16[2,32,1024]{2,1,0:T(8,128)(2,1)S(1)}, bf16[2,32,1024]{2,1,0:T(8,128)(2,1)S(1)}, u32[]{:S(2)}, u32[]{:S(2)}) %collective-permute-start.1) | collective-permute-done | bytes 131104 | tf_op jit(solution)/shard_map/ppermute | solution.py:27
  18.1 4.7 %fusion.21 = f32[128,4096]{1,0:T(8,128)S(1)} fusion(bf16[128,1024]{1,0:T(8,128)(2,1)S(1)} %bitcast.146, bf16[1024,4096]{1,0:T(8,128)(2,1)} %param.8), kind=kOutput, calls=%fused_computation.97 | convolution fusion | flops 1073741824 | bytes 10747904 | tf_op jit(solution)/shard_map/dot_general | solution.py:50
  22.9 1.7 collective-permute-start.9
  24.6 4.7 %fusion.20 = f32[128,4096]{1,0:T(8,128)S(1)} fusion(bf16[128,1024]{1,0:T(8,128)(2,1)S(1)} %bitcast.143, bf16[1024,4096]{1,0:T(8,128)(2,1)} %param.8), kind=kOutput, calls=%fused_computation.96 | convolution fusion | flops 1073741824 | bytes 10747904 | tf_op jit(solution)/shard_map/dot_general | solution.py:50
  29.3 1.9 add.267
  31.4 1.6 collective-permute-start.4
  32.9 1.5 collective-permute-start.5
  34.9 1.0 collective-permute-start.8
  36.0 2.0 collective-permute-start.7
  38.0 8.1 %collective-permute-done.8 = bf16[2,32,1024]{2,1,0:T(8,128)(2,1)} collective-permute-done((bf16[2,32,1024]{2,1,0:T(8,128)(2,1)S(1)}, bf16[2,32,1024]{2,1,0:T(8,128)(2,1)}, u32[]{:S(2)}, u32[]{:S(2)}) %collective-permute-start.8) | collective-permute-done | bytes 131104 | tf_op jit(solution)/shard_map/ppermute | solution.py:27
  46.0 1.1 pad_maximum_fusion.18
  47.2 1.4 multiply_reduce_fusion.1
  48.6 2.0 collective-permute-start.12
  50.6 1.5 collective-permute-start.10
  52.2 2.9 %collective-permute-done.11 = f32[32]{0:T(128)S(1)} collective-permute-done((f32[32]{0:T(128)S(1)}, f32[32]{0:T(128)S(1)}, u32[]{:S(2)}, u32[]{:S(2)}) %collective-permute-start.11) | collective-permute-done | bytes 160 | tf_op jit(solution)/shard_map/ppermute | solution.py:27
  55.0 0.9 collective-permute-done.10
  56.1 1.3 collective-permute-start.13
  57.4 1.3 collective-permute-start.14
  58.7 0.9 collective-permute-start.15
  59.8 4.8 %fusion.22 = f32[128,4096]{1,0:T(8,128)S(1)} fusion(bf16[128,1024]{1,0:T(8,128)(2,1)S(1)} %bitcast.145, bf16[1024,4096]{1,0:T(8,128)(2,1)} %param.8), kind=kOutput, calls=%fused_computation.98 | convolution fusion | flops 1073741824 | bytes 10747904 | tf_op jit(solution)/shard_map/dot_general | solution.py:50
  64.6 1.0 slice-done.1
  65.6 2.6 %fusion.23 = f32[128,4096]{1,0:T(8,128)} fusion(bf16[128,1024]{1,0:T(8,128)(2,1)S(1)} %bitcast.144, bf16[1024,4096]{1,0:T(8,128)(2,1)S(1)} %bitcast.117), kind=kOutput, calls=%fused_computation.99 | convolution fusion | flops 1073741824 | bytes 10747904 | tf_op jit(solution)/shard_map/dot_general | solution.py:50
  68.3 0.8 collective-permute-done.14
  69.3 1.5 fusion.17
  70.8 3.4 %collective-permute-done.20 = bf16[4,32,4096]{2,1,0:T(8,128)(2,1)} collective-permute-done((bf16[4,32,4096]{2,1,0:T(8,128)(2,1)}, bf16[4,32,4096]{2,1,0:T(8,128)(2,1)}, u32[]{:S(2)}, u32[]{:S(2)}) %collective-permute-start.20) | collective-permute-done | bytes 1048608 | tf_op jit(solution)/shard_map/ppermute | solution.py:24
  74.3 1.7 pad_maximum_fusion
  76.0 1.8 add.284
  77.9 1.3 collective-permute-start.17
  79.2 1.3 collective-permute-start.18
  80.6 0.9 collective-permute-start.19
  81.5 13.0 %fusion.24 = f32[256,3328]{1,0:T(8,128)S(1)} fusion(bf16[256,4096]{1,0:T(8,128)(2,1)S(1)} %bitcast.138, bf16[4096,3328]{1,0:T(8,128)(2,1)} %param.10), kind=kOutput, calls=%fused_computation.100 | convolution fusion | flops 6979321856 | bytes 32768000 | tf_op jit(solution)/shard_map/dot_general | solution.py:80
  94.7 1.7 collective-permute-start.21
  96.4 13.1 %fusion.25 = f32[256,3328]{1,0:T(8,128)S(1)} fusion(bf16[256,4096]{1,0:T(8,128)(2,1)S(1)} %bitcast.139, bf16[4096,3328]{1,0:T(8,128)(2,1)} %param.11), kind=kOutput, calls=%fused_computation.101 | convolution fusion | flops 6979321856 | bytes 32768000 | tf_op jit(solution)/shard_map/dot_general | solution.py:80
  110.1 2.9 %collective-permute-start.24 = (f32[32]{0:T(128)S(1)}, f32[32]{0:T(128)S(1)}, u32[]{:S(2)}, u32[]{:S(2)}) collective-permute-start(f32[32]{0:T(128)S(1)} %get-tuple-element.94), channel_id=1, source_target_pairs={{0,3},{1,0},{2,1},{3,2},{4,7},{5,4},{6,5},{7,6},{8,11},{9,8},{10,9... | collective-permute-start | bytes 392 | tf_op jit(solution)/shard_map/ppermute | solution.py:27
  114.3 3.1 %collective-permute-done.23 = f32[32]{0:T(128)S(1)} collective-permute-done((f32[32]{0:T(128)S(1)}, f32[32]{0:T(128)S(1)}, u32[]{:S(2)}, u32[]{:S(2)}) %collective-permute-start.23) | collective-permute-done | bytes 160 | tf_op jit(solution)/shard_map/ppermute | solution.py:27
  117.4 0.9 collective-permute-done.22
  118.7 1.6 collective-permute-start.29
  120.3 1.2 collective-permute-start.28
  122.3 1.0 pad_maximum_fusion.4
  123.3 1.5 collective-permute-start.25
  125.5 3.0 %collective-permute-done.29 = bf16[32,4096]{1,0:T(8,128)(2,1)S(1)} collective-permute-done((bf16[32,4096]{1,0:T(8,128)(2,1)S(1)}, bf16[32,4096]{1,0:T(8,128)(2,1)S(1)}, u32[]{:S(2)}, u32[]{:S(2)}) %collective-permute-start.29) | collective-permute-done | bytes 262176 | tf_op jit(solution)/shard_map/ppermute | solution.py:24
  128.5 2.7 %collective-permute-done.28 = bf16[32,4096]{1,0:T(8,128)(2,1)S(1)} collective-permute-done((bf16[32,4096]{1,0:T(8,128)(2,1)S(1)}, bf16[32,4096]{1,0:T(8,128)(2,1)S(1)}, u32[]{:S(2)}, u32[]{:S(2)}) %collective-permute-start.28) | collective-permute-done | bytes 262176 | tf_op jit(solution)/shard_map/ppermute | solution.py:24
  131.8 8.5 %collective-permute-done.25 = bf16[2,2,32,3328]{3,2,1,0:T(8,128)(2,1)S(1)} collective-permute-done((bf16[2,2,32,3328]{3,2,1,0:T(8,128)(2,1)S(1)}, bf16[2,2,32,3328]{3,2,1,0:T(8,128)(2,1)S(1)}, u32[]{:S(2)}, u32[]{:S(2)}) %collective-permute-start.25) | collective-permute-done | bytes 852000 | tf_op jit(solution)/shard_map/ppermute | solution.py:31
  140.3 0.9 add_convert_fusion.9
  141.3 5.7 %collective-permute-start.30 = (bf16[2,2,32,3328]{3,2,1,0:T(8,128)(2,1)S(1)}, bf16[2,2,32,3328]{3,2,1,0:T(8,128)(2,1)S(1)}, u32[]{:S(2)}, u32[]{:S(2)}) collective-permute-start(bf16[2,2,32,3328]{3,2,1,0:T(8,128)(2,1)S(1)} %pad_maximum_fusion.10), channel_id=1, source_target_pairs={{0,1},{3,2},{4,5},{7,6},{8,9},{11,10},{12,13},{15,14},{16,17},{19,... | collective-permute-start | bytes 2555912 | tf_op jit(solution)/shard_map/ppermute | solution.py:31
  147.8 1.3 collective-permute-start.32
  149.5 13.0 %fusion.26 = f32[256,3328]{1,0:T(8,128)S(1)} fusion(bf16[256,4096]{1,0:T(8,128)(2,1)S(1)} %bitcast.140, bf16[4096,3328]{1,0:T(8,128)(2,1)} %param.10), kind=kOutput, calls=%fused_computation.102 | convolution fusion | flops 6979321856 | bytes 32768000 | tf_op jit(solution)/shard_map/dot_general | solution.py:80
  162.5 13.1 %fusion.27 = f32[256,3328]{1,0:T(8,128)S(1)} fusion(bf16[256,4096]{1,0:T(8,128)(2,1)S(1)} %bitcast.141, bf16[4096,3328]{1,0:T(8,128)(2,1)} %param.11), kind=kOutput, calls=%fused_computation.103 | convolution fusion | flops 6979321856 | bytes 32768000 | tf_op jit(solution)/shard_map/dot_general | solution.py:80
  176.2 5.3 %collective-permute-start.34 = (bf16[2,2,32,3328]{3,2,1,0:T(8,128)(2,1)S(1)}, bf16[2,2,32,3328]{3,2,1,0:T(8,128)(2,1)S(1)}, u32[]{:S(2)}, u32[]{:S(2)}) collective-permute-start(bf16[2,2,32,3328]{3,2,1,0:T(8,128)(2,1)S(1)} %pad_maximum_fusion.11), channel_id=1, source_target_pairs={{0,1},{3,2},{4,5},{7,6},{8,9},{11,10},{12,13},{15,14},{16,17},{19,... | collective-permute-start | bytes 2555912 | tf_op jit(solution)/shard_map/ppermute | solution.py:31
  182.3 1.3 collective-permute-start.36
  183.7 8.6 %collective-permute-done.36 = bf16[1,2,32,3328]{3,2,1,0:T(8,128)(2,1)S(1)} collective-permute-done((bf16[1,2,32,3328]{3,2,1,0:T(8,128)(2,1)S(1)}, bf16[1,2,32,3328]{3,2,1,0:T(8,128)(2,1)S(1)}, u32[]{:S(2)}, u32[]{:S(2)}) %collective-permute-start.36) | collective-permute-done | bytes 426016 | tf_op jit(solution)/shard_map/ppermute | solution.py:31
  192.3 3.6 %collective-permute-done.34 = bf16[2,2,32,3328]{3,2,1,0:T(8,128)(2,1)S(1)} collective-permute-done((bf16[2,2,32,3328]{3,2,1,0:T(8,128)(2,1)S(1)}, bf16[2,2,32,3328]{3,2,1,0:T(8,128)(2,1)S(1)}, u32[]{:S(2)}, u32[]{:S(2)}) %collective-permute-start.34) | collective-permute-done | bytes 852000 | tf_op jit(solution)/shard_map/ppermute | solution.py:31
  196.2 4.4 %collective-permute-start.37 = (bf16[2,2,32,3328]{3,2,1,0:T(8,128)(2,1)S(1)}, bf16[2,2,32,3328]{3,2,1,0:T(8,128)(2,1)S(1)}, u32[]{:S(2)}, u32[]{:S(2)}) collective-permute-start(bf16[2,2,32,3328]{3,2,1,0:T(8,128)(2,1)S(1)} %pad_maximum_fusion.13), channel_id=1, source_target_pairs={{0,1},{3,2},{4,5},{7,6},{8,9},{11,10},{12,13},{15,14},{16,17},{19,... | collective-permute-start | bytes 2555912 | tf_op jit(solution)/shard_map/ppermute | solution.py:31
  201.3 1.6 bitcast_multiply_fusion.2
  202.9 11.8 %collective-permute-done.37 = bf16[2,2,32,3328]{3,2,1,0:T(8,128)(2,1)S(1)} collective-permute-done((bf16[2,2,32,3328]{3,2,1,0:T(8,128)(2,1)S(1)}, bf16[2,2,32,3328]{3,2,1,0:T(8,128)(2,1)S(1)}, u32[]{:S(2)}, u32[]{:S(2)}) %collective-permute-start.37) | collective-permute-done | bytes 852000 | tf_op jit(solution)/shard_map/ppermute | solution.py:31
  215.2 4.5 %collective-permute-start.39 = (bf16[2,2,32,3328]{3,2,1,0:T(8,128)(2,1)S(1)}, bf16[2,2,32,3328]{3,2,1,0:T(8,128)(2,1)S(1)}, u32[]{:S(2)}, u32[]{:S(2)}) collective-permute-start(bf16[2,2,32,3328]{3,2,1,0:T(8,128)(2,1)S(1)} %pad_maximum_fusion.12), channel_id=1, source_target_pairs={{0,1},{3,2},{4,5},{7,6},{8,9},{11,10},{12,13},{15,14},{16,17},{19,... | collective-permute-start | bytes 2555912 | tf_op jit(solution)/shard_map/ppermute | solution.py:31
  220.4 1.3 collective-permute-start.41
  221.9 10.0 %collective-permute-done.39 = bf16[2,2,32,3328]{3,2,1,0:T(8,128)(2,1)S(1)} collective-permute-done((bf16[2,2,32,3328]{3,2,1,0:T(8,128)(2,1)S(1)}, bf16[2,2,32,3328]{3,2,1,0:T(8,128)(2,1)S(1)}, u32[]{:S(2)}, u32[]{:S(2)}) %collective-permute-start.39) | collective-permute-done | bytes 852000 | tf_op jit(solution)/shard_map/ppermute | solution.py:31
  231.9 3.8 %collective-permute-done.41 = bf16[2,2,32,3328]{3,2,1,0:T(8,128)(2,1)S(1)} collective-permute-done((bf16[2,2,32,3328]{3,2,1,0:T(8,128)(2,1)S(1)}, bf16[2,2,32,3328]{3,2,1,0:T(8,128)(2,1)S(1)}, u32[]{:S(2)}, u32[]{:S(2)}) %collective-permute-start.41) | collective-permute-done | bytes 852000 | tf_op jit(solution)/shard_map/ppermute | solution.py:31
  236.3 1.2 copy-done
  (93 shorter events, 11.6 us)
Async XLA Ops:
  1.6 9.0 %collective-permute-start.2 = (bf16[2,32,1024]{2,1,0:T(8,128)(2,1)S(1)}, bf16[2,32,1024]{2,1,0:T(8,128)(2,1)S(1)}, u32[]{:S(2)}, u32[]{:S(2)}) collective-permute-start(bf16[2,32,1024]{2,1,0:T(8,128)(2,1)S(1)} %get-tuple-element.146), channel_id=1, source_target_pairs={{0,3},{1,0},{2,1},{3,2},{4,7},{5,4},{6,5},{7,6},{8,11},{9,8},{10,9... | collective-permute-start | bytes 393224 | tf_op jit(solution)/shard_map/ppermute | solution.py:27
  6.7 11.2 %collective-permute-start.1 = (bf16[2,32,1024]{2,1,0:T(8,128)(2,1)S(1)}, bf16[2,32,1024]{2,1,0:T(8,128)(2,1)S(1)}, u32[]{:S(2)}, u32[]{:S(2)}) collective-permute-start(bf16[2,32,1024]{2,1,0:T(8,128)(2,1)S(1)} %get-tuple-element.146), channel_id=1, source_target_pairs={{0,2},{1,3},{2,0},{3,1},{4,6},{5,7},{6,4},{7,5},{8,10},{9,11},{10,... | collective-permute-start | bytes 393224 | tf_op jit(solution)/shard_map/ppermute | solution.py:27
  6.8 11.2 %collective-permute-start = (bf16[2,32,1024]{2,1,0:T(8,128)(2,1)S(1)}, bf16[2,32,1024]{2,1,0:T(8,128)(2,1)S(1)}, u32[]{:S(2)}, u32[]{:S(2)}) collective-permute-start(bf16[2,32,1024]{2,1,0:T(8,128)(2,1)S(1)} %get-tuple-element.146), channel_id=1, source_target_pairs={{0,1},{1,2},{2,3},{3,0},{4,5},{5,6},{6,7},{7,4},{8,9},{9,10},{10,1... | collective-permute-start | bytes 393224 | tf_op jit(solution)/shard_map/ppermute | solution.py:27
  22.8 6.5 %collective-permute-start.3 = (f32[128,4096]{1,0:T(8,128)S(1)}, f32[128,4096]{1,0:T(8,128)}, u32[]{:S(2)}, u32[]{:S(2)}) collective-permute-start(f32[128,4096]{1,0:T(8,128)S(1)} %fusion.21), channel_id=1, source_target_pairs={{0,4},{4,0},{8,12},{12,8},{16,20},{20,16},{24,28},{28,24},{1,5},{5... | collective-permute-start | bytes 6291464 | tf_op jit(solution)/shard_map/ppermute | solution.py:24
  22.9 13.0 %collective-permute-start.9 = (bf16[2,32,1024]{2,1,0:T(8,128)(2,1)S(1)}, bf16[2,32,1024]{2,1,0:T(8,128)(2,1)}, u32[]{:S(2)}, u32[]{:S(2)}) collective-permute-start(bf16[2,32,1024]{2,1,0:T(8,128)(2,1)S(1)} %get-tuple-element.49), channel_id=1, source_target_pairs={{0,3},{1,0},{2,1},{3,2},{4,7},{5,4},{6,5},{7,6},{8,11},{9,8},{10,9... | collective-permute-start | bytes 393224 | tf_op jit(solution)/shard_map/ppermute | solution.py:27
  29.3 17.9 %copy-start.3 = (bf16[64,4096]{1,0:T(8,128)(2,1)S(1)}, bf16[64,4096]{1,0:T(8,128)(2,1)}, u32[]{:S(2)}) copy-start(bf16[64,4096]{1,0:T(8,128)(2,1)} %param.7) | copy-start | bytes 1572868
  31.3 24.7 %copy-start.4 = (f32[4096]{0:T(1024)S(1)}, f32[4096]{0:T(1024)}, u32[]{:S(2)}) copy-start(f32[4096]{0:T(1024)} %param.9) | copy-start | bytes 49156
  31.4 15.8 %collective-permute-start.4 = (bf16[32,4096]{1,0:T(8,128)(2,1)S(1)}, bf16[32,4096]{1,0:T(8,128)(2,1)}, u32[]{:S(2)}, u32[]{:S(2)}) collective-permute-start(bf16[32,4096]{1,0:T(8,128)(2,1)S(1)} %get-tuple-element.123), channel_id=1, source_target_pairs={{0,8},{4,12},{8,0},{12,4},{16,24},{20,28},{24,16},{28,20},{1,9},{5... | collective-permute-start | bytes 786440 | tf_op jit(solution)/shard_map/ppermute | solution.py:24
  32.9 14.2 %collective-permute-start.5 = (bf16[32,4096]{1,0:T(8,128)(2,1)S(1)}, bf16[32,4096]{1,0:T(8,128)(2,1)}, u32[]{:S(2)}, u32[]{:S(2)}) collective-permute-start(bf16[32,4096]{1,0:T(8,128)(2,1)S(1)} %get-tuple-element.122), channel_id=1, source_target_pairs={{0,16},{4,20},{8,24},{12,28},{16,0},{20,4},{24,8},{28,12},{1,17},{... | collective-permute-start | bytes 786440 | tf_op jit(solution)/shard_map/ppermute | solution.py:24
  34.4 12.7 %collective-permute-start.6 = (bf16[32,4096]{1,0:T(8,128)(2,1)S(1)}, bf16[32,4096]{1,0:T(8,128)(2,1)}, u32[]{:S(2)}, u32[]{:S(2)}) collective-permute-start(bf16[32,4096]{1,0:T(8,128)(2,1)S(1)} %get-tuple-element.121), channel_id=1, source_target_pairs={{0,24},{4,28},{8,16},{12,20},{16,8},{20,12},{24,0},{28,4},{1,25},{... | collective-permute-start | bytes 786440 | tf_op jit(solution)/shard_map/ppermute | solution.py:24
  34.9 11.1 %collective-permute-start.8 = (bf16[2,32,1024]{2,1,0:T(8,128)(2,1)S(1)}, bf16[2,32,1024]{2,1,0:T(8,128)(2,1)}, u32[]{:S(2)}, u32[]{:S(2)}) collective-permute-start(bf16[2,32,1024]{2,1,0:T(8,128)(2,1)S(1)} %get-tuple-element.49), channel_id=1, source_target_pairs={{0,2},{1,3},{2,0},{3,1},{4,6},{5,7},{6,4},{7,5},{8,10},{9,11},{10,... | collective-permute-start | bytes 393224 | tf_op jit(solution)/shard_map/ppermute | solution.py:27
  36.0 10.1 %collective-permute-start.7 = (bf16[2,32,1024]{2,1,0:T(8,128)(2,1)S(1)}, bf16[2,32,1024]{2,1,0:T(8,128)(2,1)}, u32[]{:S(2)}, u32[]{:S(2)}) collective-permute-start(bf16[2,32,1024]{2,1,0:T(8,128)(2,1)S(1)} %get-tuple-element.49), channel_id=1, source_target_pairs={{0,1},{1,2},{2,3},{3,0},{4,5},{5,6},{6,7},{7,4},{8,9},{9,10},{10,1... | collective-permute-start | bytes 393224 | tf_op jit(solution)/shard_map/ppermute | solution.py:27
  48.6 3.6 %collective-permute-start.12 = (f32[32]{0:T(128)S(1)}, f32[32]{0:T(128)S(1)}, u32[]{:S(2)}, u32[]{:S(2)}) collective-permute-start(f32[32]{0:T(128)S(1)} %get-tuple-element.96), channel_id=1, source_target_pairs={{0,3},{1,0},{2,1},{3,2},{4,7},{5,4},{6,5},{7,6},{8,11},{9,8},{10,9... | collective-permute-start | bytes 392 | tf_op jit(solution)/shard_map/ppermute | solution.py:27
  50.6 4.4 %collective-permute-start.11 = (f32[32]{0:T(128)S(1)}, f32[32]{0:T(128)S(1)}, u32[]{:S(2)}, u32[]{:S(2)}) collective-permute-start(f32[32]{0:T(128)S(1)} %get-tuple-element.96), channel_id=1, source_target_pairs={{0,2},{1,3},{2,0},{3,1},{4,6},{5,7},{6,4},{7,5},{8,10},{9,11},{10,... | collective-permute-start | bytes 392 | tf_op jit(solution)/shard_map/ppermute | solution.py:27
  50.6 5.3 %collective-permute-start.10 = (f32[32]{0:T(128)S(1)}, f32[32]{0:T(128)S(1)}, u32[]{:S(2)}, u32[]{:S(2)}) collective-permute-start(f32[32]{0:T(128)S(1)} %get-tuple-element.96), channel_id=1, source_target_pairs={{0,1},{1,2},{2,3},{3,0},{4,5},{5,6},{6,7},{7,4},{8,9},{9,10},{10,1... | collective-permute-start | bytes 392 | tf_op jit(solution)/shard_map/ppermute | solution.py:27
  56.1 12.2 %collective-permute-start.13 = (bf16[32,4096]{1,0:T(8,128)(2,1)S(1)}, bf16[32,4096]{1,0:T(8,128)(2,1)S(1)}, u32[]{:S(2)}, u32[]{:S(2)}) collective-permute-start(bf16[32,4096]{1,0:T(8,128)(2,1)S(1)} %multiply_convert_fusion.1), channel_id=1, source_target_pairs={{0,8},{4,12},{8,0},{12,4},{16,24},{20,28},{24,16},{28,20},{1,9},{5... | collective-permute-start | bytes 786440 | tf_op jit(solution)/shard_map/ppermute | solution.py:24
  57.4 11.7 %collective-permute-start.14 = (bf16[32,4096]{1,0:T(8,128)(2,1)S(1)}, bf16[32,4096]{1,0:T(8,128)(2,1)S(1)}, u32[]{:S(2)}, u32[]{:S(2)}) collective-permute-start(bf16[32,4096]{1,0:T(8,128)(2,1)S(1)} %multiply_convert_fusion.1), channel_id=1, source_target_pairs={{0,16},{4,20},{8,24},{12,28},{16,0},{20,4},{24,8},{28,12},{1,17},{... | collective-permute-start | bytes 786440 | tf_op jit(solution)/shard_map/ppermute | solution.py:24
  58.7 10.4 %collective-permute-start.15 = (bf16[32,4096]{1,0:T(8,128)(2,1)S(1)}, bf16[32,4096]{1,0:T(8,128)(2,1)S(1)}, u32[]{:S(2)}, u32[]{:S(2)}) collective-permute-start(bf16[32,4096]{1,0:T(8,128)(2,1)S(1)} %multiply_convert_fusion.1), channel_id=1, source_target_pairs={{0,24},{4,28},{8,16},{12,20},{16,8},{20,12},{24,0},{28,4},{1,25},{... | collective-permute-start | bytes 786440 | tf_op jit(solution)/shard_map/ppermute | solution.py:24
  59.7 4.9 %slice-start = ((s8[8388608]{0:T(1024)(128)(4,1)}), s8[4194304]{0:T(1024)(128)(4,1)S(1)}, s32[]{:S(2)}) async-start(s8[8388608]{0:T(1024)(128)(4,1)} %bitcast.116), calls=%async_computation | async-start | bytes 8388608
  59.8 5.8 %slice-start.1 = ((s8[8388608]{0:T(1024)(128)(4,1)}), s8[4194304]{0:T(1024)(128)(4,1)S(1)}, s32[]{:S(2)}) async-start(s8[8388608]{0:T(1024)(128)(4,1)} %bitcast.116), calls=%async_computation.1 | async-start | bytes 8388608
  68.2 7.7 %collective-permute-start.16 = (f32[128,4096]{1,0:T(8,128)}, f32[128,4096]{1,0:T(8,128)}, u32[]{:S(2)}, u32[]{:S(2)}) collective-permute-start(f32[128,4096]{1,0:T(8,128)} %fusion.23), channel_id=1, source_target_pairs={{0,4},{4,0},{8,12},{12,8},{16,20},{20,16},{24,28},{28,24},{1,5},{5... | collective-permute-start | bytes 6291464 | tf_op jit(solution)/shard_map/ppermute | solution.py:24
  70.8 3.5 %collective-permute-start.20 = (bf16[4,32,4096]{2,1,0:T(8,128)(2,1)}, bf16[4,32,4096]{2,1,0:T(8,128)(2,1)}, u32[]{:S(2)}, u32[]{:S(2)}) collective-permute-start(bf16[4,32,4096]{2,1,0:T(8,128)(2,1)} %get-tuple-element.133), channel_id=1, source_target_pairs={{0,4},{4,0},{8,12},{12,8},{16,20},{20,16},{24,28},{28,24},{1,5},{5... | collective-permute-start | bytes 3145736 | tf_op jit(solution)/shard_map/ppermute | solution.py:24
  77.9 31.8 %collective-permute-start.17 = (f32[32,4096]{1,0:T(8,128)S(1)}, f32[32,4096]{1,0:T(8,128)S(1)}, u32[]{:S(2)}, u32[]{:S(2)}) collective-permute-start(f32[32,4096]{1,0:T(8,128)S(1)} %get-tuple-element.120), channel_id=1, source_target_pairs={{0,8},{4,12},{8,0},{12,4},{16,24},{20,28},{24,16},{28,20},{1,9},{5... | collective-permute-start | bytes 1572872 | tf_op jit(solution)/shard_map/ppermute | solution.py:24
  79.2 30.6 %collective-permute-start.18 = (f32[32,4096]{1,0:T(8,128)S(1)}, f32[32,4096]{1,0:T(8,128)S(1)}, u32[]{:S(2)}, u32[]{:S(2)}) collective-permute-start(f32[32,4096]{1,0:T(8,128)S(1)} %get-tuple-element.119), channel_id=1, source_target_pairs={{0,16},{4,20},{8,24},{12,28},{16,0},{20,4},{24,8},{28,12},{1,17},{... | collective-permute-start | bytes 1572872 | tf_op jit(solution)/shard_map/ppermute | solution.py:24
  80.6 29.2 %collective-permute-start.19 = (f32[32,4096]{1,0:T(8,128)S(1)}, f32[32,4096]{1,0:T(8,128)S(1)}, u32[]{:S(2)}, u32[]{:S(2)}) collective-permute-start(f32[32,4096]{1,0:T(8,128)S(1)} %get-tuple-element.118), channel_id=1, source_target_pairs={{0,24},{4,28},{8,16},{12,20},{16,8},{20,12},{24,0},{28,4},{1,25},{... | collective-permute-start | bytes 1572872 | tf_op jit(solution)/shard_map/ppermute | solution.py:24
  94.7 23.8 %collective-permute-start.21 = (bf16[2,2,32,3328]{3,2,1,0:T(8,128)(2,1)S(1)}, bf16[2,2,32,3328]{3,2,1,0:T(8,128)(2,1)S(1)}, u32[]{:S(2)}, u32[]{:S(2)}) collective-permute-start(bf16[2,2,32,3328]{3,2,1,0:T(8,128)(2,1)S(1)} %pad_maximum_fusion.7), channel_id=1, source_target_pairs={{0,1},{3,2},{4,5},{7,6},{8,9},{11,10},{12,13},{15,14},{16,17},{19,... | collective-permute-start | bytes 2555912 | tf_op jit(solution)/shard_map/ppermute | solution.py:31
  110.1 4.2 %collective-permute-start.24 = (f32[32]{0:T(128)S(1)}, f32[32]{0:T(128)S(1)}, u32[]{:S(2)}, u32[]{:S(2)}) collective-permute-start(f32[32]{0:T(128)S(1)} %get-tuple-element.94), channel_id=1, source_target_pairs={{0,3},{1,0},{2,1},{3,2},{4,7},{5,4},{6,5},{7,6},{8,11},{9,8},{10,9... | collective-permute-start | bytes 392 | tf_op jit(solution)/shard_map/ppermute | solution.py:27
  113.0 4.4 %collective-permute-start.23 = (f32[32]{0:T(128)S(1)}, f32[32]{0:T(128)S(1)}, u32[]{:S(2)}, u32[]{:S(2)}) collective-permute-start(f32[32]{0:T(128)S(1)} %get-tuple-element.94), channel_id=1, source_target_pairs={{0,2},{1,3},{2,0},{3,1},{4,6},{5,7},{6,4},{7,5},{8,10},{9,11},{10,... | collective-permute-start | bytes 392 | tf_op jit(solution)/shard_map/ppermute | solution.py:27
  113.0 5.3 %collective-permute-start.22 = (f32[32]{0:T(128)S(1)}, f32[32]{0:T(128)S(1)}, u32[]{:S(2)}, u32[]{:S(2)}) collective-permute-start(f32[32]{0:T(128)S(1)} %get-tuple-element.94), channel_id=1, source_target_pairs={{0,1},{1,2},{2,3},{3,0},{4,5},{5,6},{6,7},{7,4},{8,9},{9,10},{10,1... | collective-permute-start | bytes 392 | tf_op jit(solution)/shard_map/ppermute | solution.py:27
  118.7 9.8 %collective-permute-start.29 = (bf16[32,4096]{1,0:T(8,128)(2,1)S(1)}, bf16[32,4096]{1,0:T(8,128)(2,1)S(1)}, u32[]{:S(2)}, u32[]{:S(2)}) collective-permute-start(bf16[32,4096]{1,0:T(8,128)(2,1)S(1)} %multiply_convert_fusion), channel_id=1, source_target_pairs={{0,24},{4,28},{8,16},{12,20},{16,8},{20,12},{24,0},{28,4},{1,25},{... | collective-permute-start | bytes 786440 | tf_op jit(solution)/shard_map/ppermute | solution.py:24
  120.3 10.9 %collective-permute-start.28 = (bf16[32,4096]{1,0:T(8,128)(2,1)S(1)}, bf16[32,4096]{1,0:T(8,128)(2,1)S(1)}, u32[]{:S(2)}, u32[]{:S(2)}) collective-permute-start(bf16[32,4096]{1,0:T(8,128)(2,1)S(1)} %multiply_convert_fusion), channel_id=1, source_target_pairs={{0,16},{4,20},{8,24},{12,28},{16,0},{20,4},{24,8},{28,12},{1,17},{... | collective-permute-start | bytes 786440 | tf_op jit(solution)/shard_map/ppermute | solution.py:24
  121.5 9.8 %collective-permute-start.27 = (bf16[32,4096]{1,0:T(8,128)(2,1)S(1)}, bf16[32,4096]{1,0:T(8,128)(2,1)S(1)}, u32[]{:S(2)}, u32[]{:S(2)}) collective-permute-start(bf16[32,4096]{1,0:T(8,128)(2,1)S(1)} %multiply_convert_fusion), channel_id=1, source_target_pairs={{0,8},{4,12},{8,0},{12,4},{16,24},{20,28},{24,16},{28,20},{1,9},{5... | collective-permute-start | bytes 786440 | tf_op jit(solution)/shard_map/ppermute | solution.py:24
  123.3 17.0 %collective-permute-start.25 = (bf16[2,2,32,3328]{3,2,1,0:T(8,128)(2,1)S(1)}, bf16[2,2,32,3328]{3,2,1,0:T(8,128)(2,1)S(1)}, u32[]{:S(2)}, u32[]{:S(2)}) collective-permute-start(bf16[2,2,32,3328]{3,2,1,0:T(8,128)(2,1)S(1)} %pad_maximum_fusion.8), channel_id=1, source_target_pairs={{0,1},{3,2},{4,5},{7,6},{8,9},{11,10},{12,13},{15,14},{16,17},{19,... | collective-permute-start | bytes 2555912 | tf_op jit(solution)/shard_map/ppermute | solution.py:31
  124.8 15.5 %collective-permute-start.26 = (bf16[2,2,32,3328]{3,2,1,0:T(8,128)(2,1)S(1)}, bf16[2,2,32,3328]{3,2,1,0:T(8,128)(2,1)S(1)}, u32[]{:S(2)}, u32[]{:S(2)}) collective-permute-start(bf16[2,2,32,3328]{3,2,1,0:T(8,128)(2,1)S(1)} %pad_maximum_fusion.9), channel_id=1, source_target_pairs={{1,2},{2,1},{5,6},{6,5},{9,10},{10,9},{13,14},{14,13},{17,18},{18,... | collective-permute-start | bytes 2555912 | tf_op jit(solution)/shard_map/ppermute | solution.py:31
  131.7 17.4 %collective-permute-start.33 = (bf16[4,32,4096]{2,1,0:T(8,128)(2,1)S(1)}, bf16[4,32,4096]{2,1,0:T(8,128)(2,1)S(1)}, u32[]{:S(2)}, u32[]{:S(2)}) collective-permute-start(bf16[4,32,4096]{2,1,0:T(8,128)(2,1)S(1)} %get-tuple-element.127), channel_id=1, source_target_pairs={{0,4},{4,0},{8,12},{12,8},{16,20},{20,16},{24,28},{28,24},{1,5},{5... | collective-permute-start | bytes 3145736 | tf_op jit(solution)/shard_map/ppermute | solution.py:24
  140.3 9.0 %copy-start.1 = (bf16[2,2,32,3328]{3,2,1,0:T(8,128)(2,1)}, bf16[2,2,32,3328]{3,2,1,0:T(8,128)(2,1)S(1)}, u32[]{:S(2)}) copy-start(bf16[2,2,32,3328]{3,2,1,0:T(8,128)(2,1)S(1)} %collective-permute-done.26) | copy-start | bytes 2555908
  141.3 34.6 %collective-permute-start.30 = (bf16[2,2,32,3328]{3,2,1,0:T(8,128)(2,1)S(1)}, bf16[2,2,32,3328]{3,2,1,0:T(8,128)(2,1)S(1)}, u32[]{:S(2)}, u32[]{:S(2)}) collective-permute-start(bf16[2,2,32,3328]{3,2,1,0:T(8,128)(2,1)S(1)} %pad_maximum_fusion.10), channel_id=1, source_target_pairs={{0,1},{3,2},{4,5},{7,6},{8,9},{11,10},{12,13},{15,14},{16,17},{19,... | collective-permute-start | bytes 2555912 | tf_op jit(solution)/shard_map/ppermute | solution.py:31
  147.1 28.9 %collective-permute-start.31 = (bf16[1,2,32,3328]{3,2,1,0:T(8,128)(2,1)}, bf16[1,2,32,3328]{3,2,1,0:T(8,128)(2,1)S(1)}, u32[]{:S(2)}, u32[]{:S(2)}) collective-permute-start(bf16[1,2,32,3328]{3,2,1,0:T(8,128)(2,1)} %add_convert_fusion.9), channel_id=1, source_target_pairs={{1,2},{2,1},{5,6},{6,5},{9,10},{10,9},{13,14},{14,13},{17,18},{18,... | collective-permute-start | bytes 1277960 | tf_op jit(solution)/shard_map/ppermute | solution.py:31
  147.8 28.2 %collective-permute-start.32 = (bf16[1,2,32,3328]{3,2,1,0:T(8,128)(2,1)S(1)}, bf16[1,2,32,3328]{3,2,1,0:T(8,128)(2,1)}, u32[]{:S(2)}, u32[]{:S(2)}) collective-permute-start(bf16[1,2,32,3328]{3,2,1,0:T(8,128)(2,1)S(1)} %add_convert_fusion.8), channel_id=1, source_target_pairs={{2,3},{1,0},{6,7},{5,4},{10,11},{9,8},{14,15},{13,12},{18,19},{17,... | collective-permute-start | bytes 1277960 | tf_op jit(solution)/shard_map/ppermute | solution.py:31
  176.2 19.8 %collective-permute-start.34 = (bf16[2,2,32,3328]{3,2,1,0:T(8,128)(2,1)S(1)}, bf16[2,2,32,3328]{3,2,1,0:T(8,128)(2,1)S(1)}, u32[]{:S(2)}, u32[]{:S(2)}) collective-permute-start(bf16[2,2,32,3328]{3,2,1,0:T(8,128)(2,1)S(1)} %pad_maximum_fusion.11), channel_id=1, source_target_pairs={{0,1},{3,2},{4,5},{7,6},{8,9},{11,10},{12,13},{15,14},{16,17},{19,... | collective-permute-start | bytes 2555912 | tf_op jit(solution)/shard_map/ppermute | solution.py:31
  181.6 2.1 collective-permute-start.35
  182.3 10.0 %collective-permute-start.36 = (bf16[1,2,32,3328]{3,2,1,0:T(8,128)(2,1)S(1)}, bf16[1,2,32,3328]{3,2,1,0:T(8,128)(2,1)S(1)}, u32[]{:S(2)}, u32[]{:S(2)}) collective-permute-start(bf16[1,2,32,3328]{3,2,1,0:T(8,128)(2,1)S(1)} %get-tuple-element.80), channel_id=1, source_target_pairs={{2,3},{1,0},{6,7},{5,4},{10,11},{9,8},{14,15},{13,12},{18,19},{17,... | collective-permute-start | bytes 1277960 | tf_op jit(solution)/shard_map/ppermute | solution.py:31
  183.6 17.8 %copy-start.2 = (bf16[2,2,32,3328]{3,2,1,0:T(8,128)(2,1)S(1)}, bf16[2,2,32,3328]{3,2,1,0:T(8,128)(2,1)}, u32[]{:S(2)}) copy-start(bf16[2,2,32,3328]{3,2,1,0:T(8,128)(2,1)} %copy-done.1) | copy-start | bytes 2555908
  196.2 18.5 %collective-permute-start.37 = (bf16[2,2,32,3328]{3,2,1,0:T(8,128)(2,1)S(1)}, bf16[2,2,32,3328]{3,2,1,0:T(8,128)(2,1)S(1)}, u32[]{:S(2)}, u32[]{:S(2)}) collective-permute-start(bf16[2,2,32,3328]{3,2,1,0:T(8,128)(2,1)S(1)} %pad_maximum_fusion.13), channel_id=1, source_target_pairs={{0,1},{3,2},{4,5},{7,6},{8,9},{11,10},{12,13},{15,14},{16,17},{19,... | collective-permute-start | bytes 2555912 | tf_op jit(solution)/shard_map/ppermute | solution.py:31
  200.6 14.1 %collective-permute-start.38 = (bf16[2,2,32,3328]{3,2,1,0:T(8,128)(2,1)S(1)}, bf16[2,2,32,3328]{3,2,1,0:T(8,128)(2,1)S(1)}, u32[]{:S(2)}, u32[]{:S(2)}) collective-permute-start(bf16[2,2,32,3328]{3,2,1,0:T(8,128)(2,1)S(1)} %pad_maximum_fusion.14), channel_id=1, source_target_pairs={{1,2},{2,1},{5,6},{6,5},{9,10},{10,9},{13,14},{14,13},{17,18},{18,... | collective-permute-start | bytes 2555912 | tf_op jit(solution)/shard_map/ppermute | solution.py:31
  215.2 16.7 %collective-permute-start.39 = (bf16[2,2,32,3328]{3,2,1,0:T(8,128)(2,1)S(1)}, bf16[2,2,32,3328]{3,2,1,0:T(8,128)(2,1)S(1)}, u32[]{:S(2)}, u32[]{:S(2)}) collective-permute-start(bf16[2,2,32,3328]{3,2,1,0:T(8,128)(2,1)S(1)} %pad_maximum_fusion.12), channel_id=1, source_target_pairs={{0,1},{3,2},{4,5},{7,6},{8,9},{11,10},{12,13},{15,14},{16,17},{19,... | collective-permute-start | bytes 2555912 | tf_op jit(solution)/shard_map/ppermute | solution.py:31
  219.7 12.2 %collective-permute-start.40 = (bf16[2,2,32,3328]{3,2,1,0:T(8,128)(2,1)S(1)}, bf16[2,2,32,3328]{3,2,1,0:T(8,128)(2,1)S(1)}, u32[]{:S(2)}, u32[]{:S(2)}) collective-permute-start(bf16[2,2,32,3328]{3,2,1,0:T(8,128)(2,1)S(1)} %pad_maximum_fusion.15), channel_id=1, source_target_pairs={{1,2},{2,1},{5,6},{6,5},{9,10},{10,9},{13,14},{14,13},{17,18},{18,... | collective-permute-start | bytes 2555912 | tf_op jit(solution)/shard_map/ppermute | solution.py:31
  220.4 15.2 %collective-permute-start.41 = (bf16[2,2,32,3328]{3,2,1,0:T(8,128)(2,1)S(1)}, bf16[2,2,32,3328]{3,2,1,0:T(8,128)(2,1)S(1)}, u32[]{:S(2)}, u32[]{:S(2)}) collective-permute-start(bf16[2,2,32,3328]{3,2,1,0:T(8,128)(2,1)S(1)} %pad_maximum_fusion.16), channel_id=1, source_target_pairs={{2,3},{1,0},{6,7},{5,4},{10,11},{9,8},{14,15},{13,12},{18,19},{17,... | collective-permute-start | bytes 2555912 | tf_op jit(solution)/shard_map/ppermute | solution.py:31
  236.3 1.2 copy-start
